TPU v7x, 128 devices: a whole 4x4x4 slice. The times are simulated.
128 devices in a mesh: band: 16 (over x, y), slab: 8 (over z, core).
Axes of the slice: x: 4, y: 4, z: 4, core: 2. Of those that a mesh axis runs over, the one named last changes fastest.
Arguments:
- orbitals: bfloat16 [2, 128, 64, 240, 128], P(None, ('band', 'slab')), may hold values from -6 to 6
- potential: float32 [8, 30, 16, 512], P('slab', None, 'band'), may hold values from -1.5 to 1.5
- projector: bfloat16 [8, 30, 16, 4, 64, 512], P('slab', None, 'band'), may hold values from -0.046875 to 0.046875
- block_group: int32 [8, 30, 16, 4], P('slab', None, 'band'), may hold values from 0 to 15, all different within a row
- strengths: float32 [128, 8, 8], replicated, may hold values from -4 to 4
Outputs:
- applied: bfloat16 [2, 128, 64, 240, 128], P(None, ('band', 'slab'))
Inputs may be any that keep to these rules, and one draw needn't show every extreme that they name: `block_group`: the 4 entries of one brick name different atom groups; every group is named by some brick.
All inputs are finite; a program needn't handle non-finite values.
Results may differ from a plain program's by a relative error of at most 0.012.
Values may be sent and summed in bfloat16 or wider, within the bound.
No kernel may reach another device: no remote copies, remote signals or barrier semaphores. Data moves between devices by JAX's collectives and lax.ppermute only.
A program may use at most 256 MiB of HBM per device.

v0:
```python
import math

import jax
import jax.numpy as jnp
from jax import lax
from jax.sharding import PartitionSpec as P

X = 240
Y = 128
BE = 8
P_SIZE = 512
L = 1
KB = 4
C = 64
PROJ = 8


KINETIC_SCALE = 8.0


def dft_table(length, orient):
    counter = jnp.arange(length, dtype=jnp.int32)
    product = counter[:, None] * counter[None, :] % length
    phases = product.astype(jnp.float32) * (2.0 * math.pi / length)
    cosine = jnp.cos(phases) / math.sqrt(length)
    sine_part = orient * jnp.sin(phases) / math.sqrt(length)
    return jnp.stack([jnp.stack([cosine, -sine_part]), jnp.stack([sine_part, cosine])]).astype(
        jnp.bfloat16
    )


def kinetic_term(spectrum):
    rows_x = spectrum.shape[-2]
    rows_y = spectrum.shape[-1]
    wave_x = jnp.arange(rows_x, dtype=jnp.int32)
    wave_x = jnp.minimum(wave_x, rows_x - wave_x).astype(jnp.float32) / rows_x
    wave_y = jnp.arange(rows_y, dtype=jnp.int32)
    wave_y = jnp.minimum(wave_y, rows_y - wave_y).astype(jnp.float32) / rows_y
    planar = KINETIC_SCALE * (wave_x[:, None] * wave_x[:, None] + wave_y[None, :] * wave_y[None, :])
    values = spectrum.astype(jnp.float32)
    widths = [(0, 0)] * (values.ndim - 3) + [(1, 1), (0, 0), (0, 0)]
    padded = jnp.pad(values, widths)
    along_z = 0.5 * (2.0 * values - padded[..., 2:, :, :] - padded[..., :-2, :, :])
    return planar * values + along_z


def on_device(orbitals, potential, projector, block_group, strengths):
    n_band = lax.axis_size("band")
    n_slab = lax.axis_size("slab")
    highest = lax.Precision.HIGHEST
    spectrum = orbitals[:, 0]
    planes = spectrum.shape[1]
    x_bricks = X // BE
    y_bricks = Y // BE // n_band
    n_bricks = L * x_bricks * y_bricks
    table_y = dft_table(Y, 1.0).reshape(2, 2, Y, n_band, y_bricks, BE)
    table_x = dft_table(X, 1.0).reshape(2, 2, X, x_bricks, BE)
    layered = spectrum.reshape(2, n_slab, L, BE, X, Y)
    across_y = jnp.einsum(
        "islexy,oiybcd->oslexbcd", layered, table_y, preferred_element_type=jnp.float32
    ).astype(jnp.bfloat16)
    outgoing = jnp.einsum(
        "oslexbcd,poxaf->bsplacefd", across_y, table_x, preferred_element_type=jnp.float32
    ).astype(jnp.bfloat16)
    outgoing = outgoing.reshape(n_band, n_slab, 2, n_bricks, P_SIZE)
    arrived = lax.all_to_all(
        outgoing.reshape(n_band * n_slab, 2, n_bricks, P_SIZE),
        ("band", "slab"),
        split_axis=0,
        concat_axis=0,
        tiled=True,
    )
    band_rows = arrived.reshape(-1, n_bricks, P_SIZE)
    width_rows = band_rows.shape[0]
    shaped_proj = projector.reshape(n_bricks, KB, C, P_SIZE)
    groups = block_group.reshape(n_bricks, KB)
    n_group = strengths.shape[0] * PROJ // C
    onehot = (groups[:, :, None] == jnp.arange(n_group, dtype=jnp.int32)[None, None, :]).astype(
        jnp.float32
    )
    partial_terms = jnp.einsum(
        "rbq,bkpq->bkpr", band_rows, shaped_proj, preferred_element_type=jnp.float32
    )
    coefficient = jnp.einsum(
        "bkpr,bkg->gpr",
        partial_terms,
        onehot,
        precision=highest,
        preferred_element_type=jnp.float32,
    )
    coefficient = coefficient.reshape(n_group * C, width_rows)
    symmetric = 0.5 * (strengths + jnp.transpose(strengths, (0, 2, 1)))
    owned = lax.psum_scatter(coefficient, ("band", "slab"), scatter_dimension=0, tiled=True)
    own_atoms = owned.shape[0] // PROJ
    first_atom = lax.axis_index(("band", "slab")) * own_atoms
    own_strength = lax.dynamic_slice_in_dim(symmetric, first_atom, own_atoms, 0)
    scaled = jnp.einsum(
        "aji,ajr->air",
        own_strength,
        owned.reshape(own_atoms, PROJ, width_rows),
        precision=highest,
        preferred_element_type=jnp.float32,
    ).astype(jnp.bfloat16)
    coupled = lax.all_gather(
        scaled.reshape(own_atoms * PROJ, width_rows), ("band", "slab"), axis=0, tiled=True
    )
    picked = jnp.einsum(
        "gpr,bkg->bkpr",
        coupled.reshape(n_group, C, width_rows),
        onehot.astype(jnp.bfloat16),
        preferred_element_type=jnp.float32,
    ).astype(jnp.bfloat16)
    projected = jnp.einsum(
        "bkpr,bkpq->rbq", picked, shaped_proj, preferred_element_type=jnp.float32
    )
    acted = (
        potential.reshape(n_bricks, P_SIZE)[None] * band_rows.astype(jnp.float32) + projected
    ).astype(jnp.bfloat16)
    returned = lax.all_to_all(
        acted.reshape(n_band * n_slab, 2, n_bricks, P_SIZE),
        ("band", "slab"),
        split_axis=0,
        concat_axis=0,
        tiled=True,
    )
    grid_back = returned.reshape(n_band, n_slab, 2, L, x_bricks, y_bricks, BE, BE, BE)
    back_x = dft_table(X, -1.0).reshape(2, 2, x_bricks, BE, X)
    forward_y = dft_table(Y, -1.0)
    halfway = jnp.einsum(
        "bsilacefd,oiafk->oslekbcd", grid_back, back_x, preferred_element_type=jnp.float32
    ).astype(jnp.bfloat16)
    halfway = halfway.reshape(2, planes, X, Y)
    result = jnp.einsum(
        "izxy,oiyk->ozxk", halfway, forward_y, preferred_element_type=jnp.float32
    ) + kinetic_term(spectrum)
    return result.astype(jnp.bfloat16)[:, None]


def solution(mesh):
    in_specs = (
        P(None, ("band", "slab"), None, None, None),
        P("slab", None, "band", None),
        P("slab", None, "band", None, None, None),
        P("slab", None, "band", None),
        P(),
    )
    out_specs = P(None, ("band", "slab"), None, None, None)
    return jax.shard_map(
        on_device, mesh=mesh, in_specs=in_specs, out_specs=out_specs, check_vma=False
    )
```

profile of v0, /device:TPU:1, one launch (start us, length us, event | category | flops | bytes accessed | tf_op | source)
XLA Modules:
  0.0 1381.3 jit_solution(12796635401271781320)
XLA Ops:
  6.5 0.0 reduce-scatter.2.cloned.1.call-start
  6.6 0.0 copy-start
  6.6 0.3 negate_convert_fusion.2
  6.9 0.2 copy-done
  7.1 1.2 negate_convert_fusion.1
  8.4 8.9 fusion.7
  17.2 152.6 %fusion = bf16[16,8,2,1,30,1,8,8,8]{0,7,8,6,1,4,2,5,3:T(8,128)(2,1)} fusion(bf16[2,8,8,240,16,8,1,1]{3,5,2,1,4,0,7,6:T(8,128)(2,1)} %fusion.7, bf16[1,1,240,30,8]{2,4,1,3,0:T(8,128)(2,1)S(1)} %get-tuple-element.9, bf16[1,1,240,30,8]{2,4,1,3,0:T(8,128)(2,1)S(1)} %get-tuple-element.8, bf16[1,1,240,30,8]{2,4,1,3,0:T(8,128)(2,1)S(1)} %get-tuple-element.7), kind=kOutput, calls=%fused_computation.1 | convolution fusion | flops 3780648960 | bytes 16074240 | tf_op jit(solution)/shard_map/oslexbcd,poxaf->bsplacefd/dot_general | solution.py:62
  169.8 102.8 %copy.67 = bf16[16,8,2,1,30,1,8,8,8]{4,8,7,6,2,1,0,5,3:T(8,128)(2,1)} copy(bf16[16,8,2,1,30,1,8,8,8]{0,7,8,6,1,4,2,5,3:T(8,128)(2,1)} %fusion) | data formatting | bytes 15728640 | tf_op jit(solution)/shard_map/convert_element_type | solution.py:64
  272.6 35.3 %copy.68 = bf16[128,2,30,512]{3,1,2,0:T(2,128)(2,1)} copy(bf16[128,2,30,512]{2,3,1,0:T(8,128)(2,1)} %bitcast.153) | data formatting | bytes 15728640 | tf_op jit(solution)/shard_map/reshape;reshape | solution.py:67
  307.9 104.1 %all_to_all.10 = bf16[128,2,30,512]{3,1,2,0:T(2,128)(2,1)S(1)} all-to-all(bf16[128,2,30,512]{3,1,2,0:T(2,128)(2,1)} %copy.68), channel_id=1, replica_groups=mesh['band'=16,'slab'=8] {'band','slab'}, dimensions={0} | all-to-all | bytes 15728640 | tf_op jit(solution)/shard_map/all_to_all | solution.py:66
  412.0 6.5 copy.69
  418.5 12.5 reshape.424
  430.9 0.0 copy-start.4
  430.9 10.9 fusion.19
  441.8 0.0 copy-start.2
  441.8 0.0 copy-start.3
  441.8 0.0 copy-done.4
  441.8 10.5 fusion.24
  452.4 1.7 copy.72
  454.1 0.0 reduce-scatter.2.cloned.1.call-update
  454.1 0.0 copy-done.2
  454.1 0.0 copy-done.3
  454.1 0.2 fusion.80
  454.3 12.5 reshape.409
  466.8 618.8 %reduce-scatter.2.cloned.1.call-done = f32[8,256]{1,0:T(8,128)} async-done(((f32[1024,256]{1,0:T(8,128)}), f32[8,256]{1,0:T(8,128)}) %reduce-scatter.2.cloned.1.call-update) | async-done | bytes 8208 | tf_op jit(solution)/shard_map/reduce_scatter | solution.py:93
  1085.5 0.9 convolution_convert_fusion.1
  1086.4 40.0 %all_gather.3 = bf16[1024,256]{1,0:T(8,128)(2,1)S(1)} all-gather(bf16[8,256]{1,0:T(8,128)(2,1)S(1)} %convolution_convert_fusion.1), channel_id=1, replica_groups=mesh['band'=16,'slab'=8] {'band','slab'}, dimensions={0}, use_global_device_ids=true | all-gather | bytes 528384 | tf_op jit(solution)/shard_map/all_gather | solution.py:104
  1126.4 3.3 convolution_convert_fusion
  1129.7 18.6 %fusion.5 = bf16[256,30,512]{2,0,1:T(8,128)(2,1)} fusion(bf16[256,30,512]{2,0,1:T(8,128)(2,1)} %reshape.409, bf16[1,30,1,4,64,512]{5,4,3,2,1,0:T(8,128)(2,1)} %param.7, f32[30,512]{1,0:T(8,128)S(1)} %bitcast.160, bf16[30,4,64,256]{3,0,2,1:T(8,128)(2,1)} %convolution_convert_fusion), kind=kOutput, calls=%fused_computation.10 | convolution fusion | flops 2028994560 | bytes 27586560 | tf_op jit(solution)/shard_map/bkpr,bkpq->rbq/dot_general | solution.py:113
  1148.3 12.5 reshape.414
  1160.8 7.7 copy.75
  1168.5 0.0 copy-start.1
  1168.5 6.5 all-to-all-start.1
  1175.0 0.0 copy-done.1
  1175.0 0.1 copy.64
  1175.1 0.3 fusion.77
  1175.3 0.3 negate_convert_fusion.3
  1175.6 0.1 add_multiply_fusion
  1175.7 1.3 negate_convert_fusion
  1177.1 9.9 bitcast_convert_fusion.3
  1187.0 81.4 %all-to-all-done.1 = bf16[128,2,30,512]{3,1,2,0:T(2,128)(2,1)} async-done(((bf16[128,2,30,512]{3,1,2,0:T(2,128)(2,1)}), bf16[128,2,30,512]{3,1,2,0:T(2,128)(2,1)}, u32[]{:S(2)}, u32[]{:S(2)}) %all-to-all-start.1) | async-done | bytes 7864352 | tf_op jit(solution)/shard_map/all_to_all | solution.py:119
  1268.4 34.4 %copy.76 = bf16[128,2,30,512]{2,3,1,0:T(8,128)(2,1)} copy(bf16[128,2,30,512]{3,1,2,0:T(2,128)(2,1)} %all-to-all-done.1) | data formatting | bytes 15728640 | tf_op jit(solution)/shard_map/all_to_all | solution.py:119
  1302.8 33.5 %fusion.6 = bf16[2,8,1,8,240,16,1,8]{4,5,7,3,1,0,6,2:T(8,128)(2,1)} fusion(bf16[16,8,2,30,8,8,8]{3,6,5,4,2,1,0:T(8,128)(2,1)} %bitcast.154, bf16[1,1,30,8,240]{4,2,1,3,0:T(8,128)(2,1)S(1)} %get-tuple-element.15, bf16[1,1,30,8,240]{4,2,1,3,0:T(8,128)(2,1)S(1)} %get-tuple-element.14, bf16[1,1,30,8,240]{4,2,1,3,0:T(8,128)(2,1)S(1)} %get-tuple-element.13), kind=kOutput, calls=%fused_computation.11 | convolution fusion | flops 3780648960 | bytes 16074240 | tf_op jit(solution)/shard_map/bsilacefd,oiafk->oslekbcd/dot_general | solution.py:129
  1336.3 12.2 copy.78
  1348.5 25.5 %fusion.15 = bf16[2,1,64,240,128]{4,3,2,1,0:T(8,128)(2,1)} fusion(f32[2,64,240,128]{3,2,1,0:T(8,128)} %bitcast_convert_fusion.3, f32[240,128]{1,0:T(8,128)S(1)} %add_multiply_fusion, bf16[2,64,240,128,1]{2,3,1,0,4:T(8,128)(2,1)} %bitcast.155, bf16[1,2,128,128]{3,2,1,0:T(8,128)(2,1)S(1)} %get-tuple-element.6, bf16[1,2,128,128]{3,2,1,0:T(8,128)(2,1)S(1)} %get-tuple-element.5), kind=kOutput, calls=%fused_computation.21 | convolution fusion | flops 2044985344 | bytes 31711232 | tf_op jit(solution)/shard_map/izxy,oiyk->ozxk/dot_general | solution.py:133
  (7 shorter events, 0.1 us)
Async XLA Ops:
  6.5 1079.0 %reduce-scatter.2.cloned.1.call-start = ((), (), s32[]{:S(2)}) async-start(), calls=%async_computation.3 | async-start | bytes 1056768 | tf_op jit(solution)/shard_map/reduce_scatter | solution.py:93
  6.6 0.6 copy-start
  430.9 10.9 copy-start.4
  441.8 12.3 copy-start.2
  441.8 12.3 copy-start.3
  1168.5 6.5 copy-start.1
  1168.5 99.9 %all-to-all-start.1 = ((bf16[128,2,30,512]{3,1,2,0:T(2,128)(2,1)}), bf16[128,2,30,512]{3,1,2,0:T(2,128)(2,1)}, u32[]{:S(2)}, u32[]{:S(2)}) async-start(bf16[128,2,30,512]{3,1,2,0:T(2,128)(2,1)} %copy.75), calls=%async_computation.2 | async-start | bytes 15728640 | tf_op jit(solution)/shard_map/all_to_all | solution.py:119
Sparse Core Ops, SparseCore 0:
  454.2 631.2 reduce-scatter.1
where the time goes:
time: 1400 us; the launch traced here: 1380 us
  waiting for transfers between devices  700 us (50%)
  matrix products  265 us (19%)
  local copies, waits for them, and re-layouts  238 us (17%)
  blocking collectives  144 us (10%)
  between operations  14 us (1%)
    reduce_scatter x1, waiting for transfers between devices, on_device(): lax.psum_scatter(coefficient, ('band', 'slab'), scatter_dimension=0, tile...  619 us
    dot_general x1, matrix products, on_device(): jnp.einsum('oslexbcd,poxaf->bsplacefd', across_y, table_x, preferred_elem...  153 us
    all_to_all x1, blocking collectives, on_device(): lax.all_to_all(outgoing.reshape(n_band * n_slab, 2, n_bricks, P_SIZE), ('...  104 us
    convert_element_type x1, local copies, waits for them, and re-layouts, on_device(): outgoing = jnp.einsum('oslexbcd,poxaf->bsplacefd', across_y, table_x, pre...  103 us
    all_to_all x1, waiting for transfers between devices, on_device(): lax.all_to_all(acted.reshape(n_band * n_slab, 2, n_bricks, P_SIZE), ('ban...  81.4 us
    all_gather x1, blocking collectives, on_device(): lax.all_gather(scaled.reshape(own_atoms * PROJ, width_rows), ('band', 'sl...  40 us
    another operation x1, local copies, waits for them, and re-layouts, on_device(): outgoing.reshape(n_band * n_slab, 2, n_bricks, P_SIZE)  35.3 us
    all_to_all x1, local copies, waits for them, and re-layouts, on_device(): lax.all_to_all(acted.reshape(n_band * n_slab, 2, n_bricks, P_SIZE), ('ban...  34.4 us
  transfers between devices with their start and end apart: 2, of which 2 were waited for; matrix products, arithmetic and copies ran while one was open for 2% of the time, Pallas kernels for 0%

commit v1 on v0

v1 whole, which is shorter than its diff:
```python
import math

import jax
import jax.numpy as jnp
import numpy as np
from jax import lax
from jax.experimental import pallas as pl
from jax.experimental.pallas import tpu as pltpu
from jax.sharding import PartitionSpec as P

X = 240
Y = 128
NZ = 64
BE = 8
P_SIZE = 512
KB = 4
C = 64
PROJ = 8
XB = X // BE
PAIRS = XB // 2
NBAND = 16
NSLAB = 8
NDEV = NBAND * NSLAB
NGROUP = 16
ROWS = 2 * NDEV
HALF = 64
KINETIC_SCALE = 8.0
AXES = ("band", "slab")
F32 = jnp.float32
BF16 = jnp.bfloat16
VMEM_LIMIT = 48 * 1024 * 1024


def cos_sin(length):
    counter = np.arange(length)
    phases = (counter[:, None] * counter[None, :] % length) * (2.0 * math.pi / length)
    return np.cos(phases) / math.sqrt(length), np.sin(phases) / math.sqrt(length)


def bf16_table(values):
    return jnp.asarray(np.asarray(values, np.float32), dtype=BF16)


def x_order():
    x = np.arange(X).reshape(XB, BE // 2, 2)
    return x.transpose(2, 0, 1).reshape(-1)


def point_order():
    q = np.arange(P_SIZE).reshape(BE, BE, BE)
    return q.transpose(1, 0, 2).reshape(-1)


def nt(a, b):
    return lax.dot_general(a, b, (((1,), (1,)), ((), ())), preferred_element_type=F32)


def nn(a, b):
    return lax.dot_general(a, b, (((1,), (0,)), ((), ())), preferred_element_type=F32)


def to_grid_kernel(spec_ref, ty_ref, tx_ref, out_ref, across_ref):
    for e in range(BE):
        plane = jnp.concatenate([spec_ref[0, 0, e], spec_ref[1, 0, e]], axis=1)
        across = nt(ty_ref[...], plane)
        across_ref[:, :, e] = across.reshape(2, NBAND, BE, X)
    low = lax.broadcasted_iota(jnp.int32, (X // 2, 128), 1) < HALF

    def column(c, carry):
        re = across_ref[0, c].reshape(BE * BE, X).astype(BF16)
        im = across_ref[1, c].reshape(BE * BE, X).astype(BF16)
        whole = nt(tx_ref[0], jnp.concatenate([re, im], axis=0)) + nt(
            tx_ref[1], jnp.concatenate([-im, re], axis=0)
        )
        even = whole[: X // 2]
        odd = whole[X // 2 :]
        first = jnp.where(low, even, pltpu.roll(odd, HALF, 1))
        second = jnp.where(low, pltpu.roll(even, HALF, 1), odd)
        rows = jnp.stack(
            [first.reshape(PAIRS, 8, 128), second.reshape(PAIRS, 8, 128)], axis=1
        ).reshape(X, 128)
        out_ref[c, 0] = rows.astype(BF16)
        return carry

    lax.fori_loop(0, NBAND, column, 0, unroll=2)


def to_grid(orbitals):
    cy, sy = cos_sin(Y)
    ty = bf16_table(np.block([[cy, -sy], [sy, cy]]))
    cx, sx = cos_sin(X)
    order = x_order()
    tx = bf16_table(np.stack([cx[order], sx[order]]))
    return pl.pallas_call(
        to_grid_kernel,
        grid=(NSLAB,),
        in_specs=[
            pl.BlockSpec((2, 1, BE, X, Y), lambda s: (0, 0, s, 0, 0)),
            pl.BlockSpec((2 * Y, 2 * Y), lambda s: (0, 0)),
            pl.BlockSpec((2, X, X), lambda s: (0, 0, 0)),
        ],
        out_specs=pl.BlockSpec((NBAND, 1, X, 128), lambda s: (0, s, 0, 0)),
        out_shape=jax.ShapeDtypeStruct((NBAND, NSLAB, X, 128), BF16),
        scratch_shapes=[pltpu.VMEM((2, NBAND, BE, BE, X), F32)],
        compiler_params=pltpu.CompilerParams(vmem_limit_bytes=VMEM_LIMIT),
        name="to_grid",
    )(orbitals, ty, tx)


def project_kernel(groups_ref, bricks_ref, proj_ref, rows_ref, sums_ref, wide_ref, coef_ref):
    t = pl.program_id(0)

    @pl.when(t == 0)
    def _():
        coef_ref[...] = jnp.zeros_like(coef_ref)

    wide_ref[...] = bricks_ref[...].astype(F32).reshape(NDEV * 16, 128)
    for low in range(2):
        for part in range(2):
            for high in range(4):
                j = part * 8 + low * 4 + high
                piece = wide_ref[pl.ds(j, NDEV, stride=16), :]
                rows_ref[low, pl.ds(part * NDEV, NDEV), pl.ds(high * 128, 128)] = piece.astype(BF16)
        partial = nt(proj_ref[low], rows_ref[low])
        for k in range(KB):
            g = groups_ref[(2 * t + low) * KB + k]
            coef_ref[g] += partial[k * C : (k + 1) * C]

    @pl.when(t == PAIRS - 1)
    def _():
        sums_ref[...] = coef_ref[...].astype(BF16)


def project(groups, bricks, proj):
    return pl.pallas_call(
        project_kernel,
        grid_spec=pltpu.PrefetchScalarGridSpec(
            num_scalar_prefetch=1,
            grid=(PAIRS,),
            in_specs=[
                pl.BlockSpec((NDEV, 16, 128), lambda t, g: (0, t, 0)),
                pl.BlockSpec((2, KB * C, P_SIZE), lambda t, g: (t, 0, 0)),
            ],
            out_specs=[
                pl.BlockSpec((2, ROWS, P_SIZE), lambda t, g: (t, 0, 0)),
                pl.BlockSpec((NGROUP, C, ROWS), lambda t, g: (0, 0, 0)),
            ],
            scratch_shapes=[
                pltpu.VMEM((NDEV * 16, 128), F32),
                pltpu.VMEM((NGROUP, C, ROWS), F32),
            ],
        ),
        out_shape=[
            jax.ShapeDtypeStruct((XB, ROWS, P_SIZE), BF16),
            jax.ShapeDtypeStruct((NGROUP, C, ROWS), BF16),
        ],
        compiler_params=pltpu.CompilerParams(vmem_limit_bytes=VMEM_LIMIT),
        name="project",
    )(groups, bricks, proj)


def couple_kernel(sums_ref, strength_ref, out_ref):
    total = jnp.sum(sums_ref[...].astype(F32), axis=0)
    strength = 0.5 * (strength_ref[0] + strength_ref[0].T)
    scaled = strength[:, 0:1] * total[0:1]
    for j in range(1, PROJ):
        scaled = scaled + strength[:, j : j + 1] * total[j : j + 1]
    out_ref[...] = jnp.broadcast_to(scaled[None], (NDEV, PROJ, ROWS)).astype(BF16)


def couple(sums, strengths):
    return pl.pallas_call(
        couple_kernel,
        out_shape=jax.ShapeDtypeStruct((NDEV, PROJ, ROWS), BF16),
        compiler_params=pltpu.CompilerParams(vmem_limit_bytes=VMEM_LIMIT),
        name="couple",
    )(sums, strengths)


def act_kernel(groups_ref, coupled_ref, rows_ref, proj_ref, pot_ref, out_ref, picks_ref, wide_ref):
    t = pl.program_id(0)

    @pl.when(t == 0)
    def _():
        unit = (
            lax.broadcasted_iota(jnp.int32, (ROWS, ROWS), 0)
            == lax.broadcasted_iota(jnp.int32, (ROWS, ROWS), 1)
        ).astype(BF16)
        zeros = jnp.zeros((C, ROWS), BF16)
        for g in range(NGROUP):
            block = coupled_ref[g]
            picks_ref[0, g] = nt(unit, jnp.concatenate([block, zeros], axis=0)).astype(BF16)
            picks_ref[1, g] = nt(unit, jnp.concatenate([zeros, block], axis=0)).astype(BF16)

    for low in range(2):
        g = [groups_ref[(2 * t + low) * KB + k] for k in range(KB)]
        picked = jnp.concatenate(
            [picks_ref[0, g[0]] + picks_ref[1, g[1]], picks_ref[0, g[2]] + picks_ref[1, g[3]]],
            axis=1,
        )
        acted = nn(picked, proj_ref[low]) + pot_ref[low] * rows_ref[low].astype(F32)
        for part in range(2):
            for high in range(4):
                j = part * 8 + low * 4 + high
                wide_ref[pl.ds(j, NDEV, stride=16), :] = acted[
                    part * NDEV : (part + 1) * NDEV, high * 128 : (high + 1) * 128
                ]
    out_ref[...] = wide_ref[...].reshape(NDEV, 16, 128).astype(BF16)


def act(groups, coupled, rows, proj, pot):
    return pl.pallas_call(
        act_kernel,
        grid_spec=pltpu.PrefetchScalarGridSpec(
            num_scalar_prefetch=1,
            grid=(PAIRS,),
            in_specs=[
                pl.BlockSpec((NGROUP, C, ROWS), lambda t, g: (0, 0, 0)),
                pl.BlockSpec((2, ROWS, P_SIZE), lambda t, g: (t, 0, 0)),
                pl.BlockSpec((2, KB * C, P_SIZE), lambda t, g: (t, 0, 0)),
                pl.BlockSpec((2, 1, P_SIZE), lambda t, g: (t, 0, 0)),
            ],
            out_specs=pl.BlockSpec((NDEV, 16, 128), lambda t, g: (0, t, 0)),
            scratch_shapes=[
                pltpu.VMEM((2, NGROUP, ROWS, 2 * C), BF16),
                pltpu.VMEM((NDEV * 16, 128), F32),
            ],
        ),
        out_shape=jax.ShapeDtypeStruct((NDEV, X, 128), BF16),
        compiler_params=pltpu.CompilerParams(vmem_limit_bytes=VMEM_LIMIT),
        name="act",
    )(groups, coupled, rows, proj, pot)


def to_waves_kernel(
    grid_ref, spec_ref, below_ref, above_ref, unit_ref, tx_ref, ty_ref, planar_ref, out_ref, turned_ref
):
    s = pl.program_id(0)

    def turn(c, carry):
        turned = nt(unit_ref[...], grid_ref[c, 0])
        turned_ref[:, :, c] = turned.reshape(2, BE, BE, X)
        return carry

    lax.fori_loop(0, NBAND, turn, 0, unroll=2)
    has_below = (s > 0).astype(F32)
    has_above = (s < NSLAB - 1).astype(F32)
    for e in range(BE):
        even = turned_ref[0, e].reshape(Y, X).astype(BF16)
        odd = turned_ref[1, e].reshape(Y, X).astype(BF16)
        half = nt(tx_ref[0], even) + nt(tx_ref[1], odd)
        half = jnp.concatenate([half[:X], half[X:]], axis=1).astype(BF16)
        result = nn(half, ty_ref[...])
        for o in range(2):
            here = spec_ref[o, 0, e].astype(F32)
            if e == 0:
                below = below_ref[o, 0, 0].astype(F32) * has_below
            else:
                below = spec_ref[o, 0, e - 1].astype(F32)
            if e == BE - 1:
                above = above_ref[o, 0, 0].astype(F32) * has_above
            else:
                above = spec_ref[o, 0, e + 1].astype(F32)
            kinetic = planar_ref[...] * here + 0.5 * (2.0 * here - above - below)
            out_ref[o, 0, e] = (result[:, o * Y : (o + 1) * Y] + kinetic).astype(BF16)


def to_waves(grid, orbitals):
    cx, sx = cos_sin(X)
    x = np.arange(X).reshape(PAIRS, 2, BE // 2, 2)
    tables = []
    for low in range(2):
        own = x[..., low].reshape(PAIRS, 8)
        re, im = np.zeros((2 * X, PAIRS, 8)), np.zeros((2 * X, PAIRS, 8))
        re[:X], re[X:] = cx[:, own], -sx[:, own]
        im[:X], im[X:] = sx[:, own], cx[:, own]
        tables.append(np.stack([re, im], axis=2).reshape(2 * X, X))
    tx = bf16_table(np.stack(tables))
    cy, sy = cos_sin(Y)
    ty = bf16_table(np.block([[cy, -sy], [sy, cy]]))
    wave_x = np.minimum(np.arange(X), X - np.arange(X)).astype(np.float32) / X
    wave_y = np.minimum(np.arange(Y), Y - np.arange(Y)).astype(np.float32) / Y
    planar = jnp.asarray(
        KINETIC_SCALE * (wave_x[:, None] * wave_x[:, None] + wave_y[None, :] * wave_y[None, :]), dtype=F32
    )
    return pl.pallas_call(
        to_waves_kernel,
        grid=(NSLAB,),
        in_specs=[
            pl.BlockSpec((NBAND, 1, X, 128), lambda s: (0, s, 0, 0)),
            pl.BlockSpec((2, 1, BE, X, Y), lambda s: (0, 0, s, 0, 0)),
            pl.BlockSpec((2, 1, 1, X, Y), lambda s: (0, 0, jnp.maximum(s * BE - 1, 0), 0, 0)),
            pl.BlockSpec((2, 1, 1, X, Y), lambda s: (0, 0, jnp.minimum(s * BE + BE, NZ - 1), 0, 0)),
            pl.BlockSpec((128, 128), lambda s: (0, 0)),
            pl.BlockSpec((2, 2 * X, X), lambda s: (0, 0, 0)),
            pl.BlockSpec((2 * Y, 2 * Y), lambda s: (0, 0)),
            pl.BlockSpec((X, Y), lambda s: (0, 0)),
        ],
        out_specs=pl.BlockSpec((2, 1, BE, X, Y), lambda s: (0, 0, s, 0, 0)),
        out_shape=jax.ShapeDtypeStruct((2, 1, NZ, X, Y), BF16),
        scratch_shapes=[pltpu.VMEM((2, BE, NBAND, BE, X), F32)],
        compiler_params=pltpu.CompilerParams(vmem_limit_bytes=VMEM_LIMIT),
        name="to_waves",
    )(grid, orbitals, orbitals, orbitals, bf16_table(np.eye(128)), tx, ty, planar)


def exchange(array):
    return lax.all_to_all(array, AXES, split_axis=0, concat_axis=0, tiled=True)


def on_device(orbitals, potential, projector, block_group, strengths):
    groups = block_group.reshape(-1)
    order = point_order()
    turn = np.zeros((P_SIZE, P_SIZE), np.float32)
    turn[order, np.arange(P_SIZE)] = 1.0
    proj = nn(projector.reshape(XB * KB * C, P_SIZE), jnp.asarray(turn, dtype=BF16)).astype(BF16)
    proj = proj.reshape(XB, KB * C, P_SIZE)
    pot = potential.reshape(XB, BE, BE, BE).transpose(0, 2, 1, 3).reshape(XB, 1, P_SIZE)
    own = lax.axis_index(AXES)
    strength = lax.dynamic_slice_in_dim(strengths, own, 1, 0)

    bricks = exchange(to_grid(orbitals).reshape(NDEV, X, 128))
    rows, sums = project(groups, bricks, proj)
    coupled = exchange(couple(exchange(sums.reshape(NDEV, PROJ, ROWS)), strength))
    acted = act(groups, coupled.reshape(NGROUP, C, ROWS), rows, proj, pot)
    returned = exchange(acted).reshape(NBAND, NSLAB, X, 128)
    return to_waves(returned, orbitals)


def solution(mesh):
    in_specs = (
        P(None, AXES, None, None, None),
        P("slab", None, "band", None),
        P("slab", None, "band", None, None, None),
        P("slab", None, "band", None),
        P(),
    )
    out_specs = P(None, AXES, None, None, None)
    return jax.shard_map(
        on_device, mesh=mesh, in_specs=in_specs, out_specs=out_specs, check_vma=False
    )
```

time: 1400 us -> 362 us (0.26); the launches traced: 1380 us -> 361 us
  waiting for transfers between devices: 700 us -> 99.6 us
  matrix products: 265 us -> 9.82 us
  local copies, waits for them, and re-layouts: 238 us -> 13.2 us
  Pallas kernels: 0 us -> 110 us
  blocking collectives: 144 us -> 98.5 us
  starting transfers between devices: 6.5 us -> 29.2 us
    reduce_scatter x1 -> x0, waiting for transfers between devices: 619 us -> none  [on_device(): lax.psum_scatter(coefficient, ('band', 'slab'), scatter_dimension=0, tile...]
    dot_general x9 -> x1, matrix products: 265 us -> 9.82 us  [nn(): lax.dot_general(a, b, (((1,), (0,)), ((), ())), preferred_element_type=F32)]
    pallas_call x0 -> x5, Pallas kernels: none -> 110 us  [the longest x1 42.3 us: to_waves(): pl.pallas_call(to_waves_kernel, grid=(NSLAB,), in_specs=[pl.BlockSpec((NB...]
    convert_element_type x2 -> x1, local copies, waits for them, and re-layouts: 115 us -> 10.7 us  [on_device(): nn(projector.reshape(XB * KB * C, P_SIZE), jnp.asarray(turn, dtype=BF16))]
    reshape x4 -> x2, local copies, waits for them, and re-layouts: 45 us -> 0.22 us  [the longest x1 0.12 us: on_device(): potential.reshape(XB, BE, BE, BE).transpose(0, 2, 1, 3)]
    all_to_all x2 -> x0, local copies, waits for them, and re-layouts: 40.9 us -> none  [the longest x1 34.4 us: on_device(): lax.all_to_all(acted.reshape(n_band * n_slab, 2, n_bricks, P_SIZE), ('ban...]
    all_gather x1 -> x0, blocking collectives: 40 us -> none  [on_device(): lax.all_gather(scaled.reshape(own_atoms * PROJ, width_rows), ('band', 'sl...]
    another operation x1 -> x0, local copies, waits for them, and re-layouts: 35.3 us -> none  [on_device(): outgoing.reshape(n_band * n_slab, 2, n_bricks, P_SIZE)]
  transfers between devices with their start and end apart: 2 -> 3, of which waited for: 2 -> 3; matrix products, arithmetic and copies ran while one was open for 2% -> 6% of each run, Pallas kernels for 0% -> 0%
where the time goes in v1:
time: 362 us; the launch traced here: 361 us
  Pallas kernels  110 us (30%)
  waiting for transfers between devices  99.6 us (28%)
  blocking collectives  98.5 us (27%)
  starting transfers between devices  29.2 us (8%)
  local copies, waits for them, and re-layouts  13.2 us (4%)
  matrix products  9.82 us (3%)
    all_to_all x3, waiting for transfers between devices, exchange(): return lax.all_to_all(array, AXES, split_axis=0, concat_axis=0, tiled=True)  99.6 us
    all_to_all x1, blocking collectives, exchange(): return lax.all_to_all(array, AXES, split_axis=0, concat_axis=0, tiled=True)  98.5 us
    pallas_call x1, Pallas kernels, to_waves(): pl.pallas_call(to_waves_kernel, grid=(NSLAB,), in_specs=[pl.BlockSpec((NB...  42.3 us
    pallas_call x1, Pallas kernels, to_grid(): pl.pallas_call(to_grid_kernel, grid=(NSLAB,), in_specs=[pl.BlockSpec((2,...  29.5 us
    all_to_all x3, starting transfers between devices, exchange(): return lax.all_to_all(array, AXES, split_axis=0, concat_axis=0, tiled=True)  29.2 us
    pallas_call x1, Pallas kernels, project(): pl.pallas_call(project_kernel, grid_spec=pltpu.PrefetchScalarGridSpec(num...  19.1 us
    pallas_call x1, Pallas kernels, act(): pl.pallas_call(act_kernel, grid_spec=pltpu.PrefetchScalarGridSpec(num_sca...  18.3 us
    convert_element_type x1, local copies, waits for them, and re-layouts, on_device(): nn(projector.reshape(XB * KB * C, P_SIZE), jnp.asarray(turn, dtype=BF16))  10.7 us
  transfers between devices with their start and end apart: 3, of which 3 were waited for; matrix products, arithmetic and copies ran while one was open for 6% of the time, Pallas kernels for 0%

profile of v1, /device:TPU:1, one launch (start us, length us, event | category | flops | bytes accessed | tf_op | source)
XLA Modules:
  0.0 360.6 jit_solution(16200547995233109973)
XLA Ops:
  0.0 0.0 copy-start
  0.0 0.0 copy-start.2
  0.0 0.9 copy-done.2
  0.9 0.0 copy-start.5
  0.9 0.9 copy-done.5
  1.9 29.5 %to_grid.1 = bf16[16,8,240,128]{3,2,1,0:T(8,128)(2,1)} custom-call(bf16[2,1,64,240,128]{4,3,2,1,0:T(8,128)(2,1)} %above_ref.1, bf16[256,256]{1,0:T(8,128)(2,1)S(1)} %copy-done.2, bf16[2,240,240]{2,1,0:T(8,128)(2,1)S(1)} %copy-done.5), custom_call_target="tpu_custom_call" | custom-call | tf_op jit(solution)/shard_map/to_grid/pallas_call | solution.py:94
  31.3 0.0 copy-start.10
  31.3 11.9 %all-to-all-start = ((bf16[128,240,128]{2,1,0:T(8,128)(2,1)}), bf16[128,240,128]{2,1,0:T(8,128)(2,1)}, u32[]{:S(2)}, u32[]{:S(2)}) async-start(bf16[128,240,128]{2,1,0:T(8,128)(2,1)} %bitcast.19), calls=%async_computation | async-start | bytes 15728640 | tf_op jit(solution)/shard_map/all_to_all | solution.py:308
  43.2 0.0 copy-done.10
  43.2 9.8 %fusion = bf16[7680,512]{0,1:T(8,128)(2,1)} fusion(bf16[512,512]{1,0:T(8,128)(2,1)S(1)} %copy-done.10, bf16[7680,512]{1,0:T(8,128)(2,1)} %bitcast.23), kind=kOutput, calls=%fused_computation.1 | convolution fusion | flops 4030464000 | bytes 16252928 | tf_op jit(solution)/shard_map/dot_general | solution.py:59
  53.1 0.0 copy-start.9
  53.1 10.7 %copy.18 = bf16[7680,512]{1,0:T(8,128)(2,1)} copy(bf16[7680,512]{0,1:T(8,128)(2,1)} %fusion) | data formatting | bytes 15728640 | tf_op jit(solution)/shard_map/convert_element_type | solution.py:316
  63.7 0.0 copy-done.9
  63.7 0.1 copy.17
  63.8 0.1 reshape.27.groups_ref
  63.9 72.7 %all-to-all-done.bricks_ref = bf16[128,240,128]{2,1,0:T(8,128)(2,1)} async-done(((bf16[128,240,128]{2,1,0:T(8,128)(2,1)}), bf16[128,240,128]{2,1,0:T(8,128)(2,1)}, u32[]{:S(2)}, u32[]{:S(2)}) %all-to-all-start) | async-done | bytes 7864352 | tf_op jit(solution)/shard_map/all_to_all | solution.py:308
  136.6 0.0 copy-start.8
  136.6 19.1 %project.1 = (bf16[30,256,512]{2,1,0:T(8,128)(2,1)}, bf16[16,64,256]{2,1,0:T(8,128)(2,1)}) custom-call(s32[120]{0:T(128)S(1)} %reshape.27.groups_ref, bf16[128,240,128]{2,1,0:T(8,128)(2,1)} %all-to-all-done.bricks_ref, bf16[30,256,512]{2,1,0:T(8,128)(2,1)} %bitcast.17), custom_call_target="tpu_custom_call" | custom-call | tf_op jit(solution)/shard_map/project/pallas_call | solution.py:135
  155.7 12.7 %all-to-all-start.1 = ((bf16[128,8,256]{2,1,0:T(8,128)(2,1)}), bf16[128,8,256]{2,1,0:T(8,128)(2,1)S(1)}, u32[]{:S(2)}, u32[]{:S(2)}) async-start(bf16[128,8,256]{2,1,0:T(8,128)(2,1)} %bitcast.4), calls=%async_computation.1 | async-start | bytes 1048576 | tf_op jit(solution)/shard_map/all_to_all | solution.py:308
  168.4 0.0 copy-done
  168.4 0.1 constant_dynamic-slice_fusion
  168.5 0.1 copy.23.strength_ref
  168.6 13.5 %all-to-all-done.1.sums_ref = bf16[128,8,256]{2,1,0:T(8,128)(2,1)S(1)} async-done(((bf16[128,8,256]{2,1,0:T(8,128)(2,1)}), bf16[128,8,256]{2,1,0:T(8,128)(2,1)S(1)}, u32[]{:S(2)}, u32[]{:S(2)}) %all-to-all-start.1) | async-done | bytes 524320 | tf_op jit(solution)/shard_map/all_to_all | solution.py:308
  182.0 1.0 couple.1
  183.1 4.6 %all-to-all-start.2 = ((bf16[128,8,256]{2,1,0:T(8,128)(2,1)}), bf16[128,8,256]{2,1,0:T(8,128)(2,1)S(1)}, u32[]{:S(2)}, u32[]{:S(2)}) async-start(bf16[128,8,256]{2,1,0:T(8,128)(2,1)} %couple.1), calls=%async_computation.2 | async-start | bytes 1048576 | tf_op jit(solution)/shard_map/all_to_all | solution.py:308
  187.7 0.0 copy-done.8
  187.7 0.1 copy.20
  187.9 0.1 copy.22.pot_ref
  188.0 13.5 %all-to-all-done.2 = bf16[128,8,256]{2,1,0:T(8,128)(2,1)S(1)} async-done(((bf16[128,8,256]{2,1,0:T(8,128)(2,1)}), bf16[128,8,256]{2,1,0:T(8,128)(2,1)S(1)}, u32[]{:S(2)}, u32[]{:S(2)}) %all-to-all-start.2) | async-done | bytes 524320 | tf_op jit(solution)/shard_map/all_to_all | solution.py:308
  201.5 18.3 %act.1 = bf16[128,240,128]{2,1,0:T(8,128)(2,1)} custom-call(s32[120]{0:T(128)S(1)} %reshape.27.groups_ref, bf16[16,64,256]{2,1,0:T(8,128)(2,1)S(1)} %bitcast.16, bf16[30,256,512]{2,1,0:T(8,128)(2,1)} %get-tuple-element.8.rows_ref, bf16[30,256,512]{2,1,0:T(8,128)(2,1)} %bitcast.18, f32[30,1,512]{2,1,0:T(1,128)S(1)} %copy.22.pot_ref), custom_call_target="tpu_custom_call" | custom-call | tf_op jit(solution)/shard_map/act/pallas_call | solution.py:212
  219.8 0.0 copy-start.3
  219.8 0.0 copy-start.4
  219.8 0.0 copy-start.6
  219.8 0.0 copy-start.7
  219.8 98.5 %all_to_all.20 = bf16[128,240,128]{2,1,0:T(8,128)(2,1)} all-to-all(bf16[128,240,128]{2,1,0:T(8,128)(2,1)} %act.1), channel_id=1, replica_groups=mesh['band'=16,'slab'=8] {'band','slab'}, dimensions={0} | all-to-all | bytes 15728640 | tf_op jit(solution)/shard_map/all_to_all | solution.py:308
  318.3 0.0 copy-done.3
  318.3 0.0 copy-done.4
  318.3 0.0 copy-done.6
  318.3 0.0 copy-done.7
  318.3 0.0 copy-start.1
  318.3 42.3 %to_waves.1 = bf16[2,1,64,240,128]{4,3,2,1,0:T(8,128)(2,1)} custom-call(bf16[16,8,240,128]{3,2,1,0:T(8,128)(2,1)} %bitcast.20, bf16[2,1,64,240,128]{4,3,2,1,0:T(8,128)(2,1)} %above_ref.1, bf16[2,1,64,240,128]{4,3,2,1,0:T(8,128)(2,1)} %above_ref.1, bf16[2,1,64,240,128]{4,3,2,1,0:T(8,128)(2,1)} %above_ref.1, bf16[128,128]{1,0:T(8,128)(2,1)S(1)} %copy-done.7, ...), custom_call_target="tpu_custom_call" | custom-call | tf_op jit(solution)/shard_map/to_waves/pallas_call | solution.py:286
  360.6 0.0 copy-done.1
  (1 shorter events, 0.0 us)
Async XLA Ops:
  0.0 168.4 %copy-start = (f32[128,8,8]{0,2,1:T(8,128)S(1)}, f32[128,8,8]{0,2,1:T(8,128)}, u32[]{:S(2)}) copy-start(f32[128,8,8]{0,2,1:T(8,128)} %param.16) | copy-start | bytes 98308
  0.0 0.9 copy-start.2
  0.9 0.9 copy-start.5
  31.3 11.9 %copy-start.10 = (bf16[512,512]{1,0:T(8,128)(2,1)S(1)}, bf16[512,512]{1,0:T(8,128)(2,1)}, u32[]{:S(2)}) copy-start(bf16[512,512]{1,0:T(8,128)(2,1)} %constant.27.clone) | copy-start | bytes 1572868
  31.3 105.3 %all-to-all-start = ((bf16[128,240,128]{2,1,0:T(8,128)(2,1)}), bf16[128,240,128]{2,1,0:T(8,128)(2,1)}, u32[]{:S(2)}, u32[]{:S(2)}) async-start(bf16[128,240,128]{2,1,0:T(8,128)(2,1)} %bitcast.19), calls=%async_computation | async-start | bytes 15728640 | tf_op jit(solution)/shard_map/all_to_all | solution.py:308
  53.1 10.7 %copy-start.9 = (s32[1,30,1,4]{1,3,2,0:T(4,128)S(1)}, s32[1,30,1,4]{1,3,2,0:T(4,128)}, u32[]{:S(2)}) copy-start(s32[1,30,1,4]{1,3,2,0:T(4,128)} %param.15) | copy-start | bytes 1444
  136.6 51.1 %copy-start.8 = (f32[1,30,1,512]{3,2,1,0:T(1,128)S(1)}, f32[1,30,1,512]{3,2,1,0:T(1,128)}, u32[]{:S(2)}) copy-start(f32[1,30,1,512]{3,2,1,0:T(1,128)} %param.13) | copy-start | bytes 184324
  155.7 26.3 %all-to-all-start.1 = ((bf16[128,8,256]{2,1,0:T(8,128)(2,1)}), bf16[128,8,256]{2,1,0:T(8,128)(2,1)S(1)}, u32[]{:S(2)}, u32[]{:S(2)}) async-start(bf16[128,8,256]{2,1,0:T(8,128)(2,1)} %bitcast.4), calls=%async_computation.1 | async-start | bytes 1048576 | tf_op jit(solution)/shard_map/all_to_all | solution.py:308
  183.1 18.4 %all-to-all-start.2 = ((bf16[128,8,256]{2,1,0:T(8,128)(2,1)}), bf16[128,8,256]{2,1,0:T(8,128)(2,1)S(1)}, u32[]{:S(2)}, u32[]{:S(2)}) async-start(bf16[128,8,256]{2,1,0:T(8,128)(2,1)} %couple.1), calls=%async_computation.2 | async-start | bytes 1048576 | tf_op jit(solution)/shard_map/all_to_all | solution.py:308
  219.8 98.5 %copy-start.3 = (bf16[256,256]{1,0:T(8,128)(2,1)S(1)}, bf16[256,256]{1,0:T(8,128)(2,1)}, u32[]{:S(2)}) copy-start(bf16[256,256]{1,0:T(8,128)(2,1)} %constant.28.clone.ty_ref) | copy-start | bytes 393220
  219.8 98.5 %copy-start.4 = (bf16[2,480,240]{2,1,0:T(8,128)(2,1)S(1)}, bf16[2,480,240]{2,1,0:T(8,128)(2,1)}, u32[]{:S(2)}) copy-start(bf16[2,480,240]{2,1,0:T(8,128)(2,1)} %constant.30.clone.tx_ref) | copy-start | bytes 1382404
  219.8 98.5 %copy-start.6 = (f32[240,128]{1,0:T(8,128)S(1)}, f32[240,128]{1,0:T(8,128)}, u32[]{:S(2)}) copy-start(f32[240,128]{1,0:T(8,128)} %constant.31.clone.planar_ref) | copy-start | bytes 368644
  219.8 98.5 %copy-start.7 = (bf16[128,128]{1,0:T(8,128)(2,1)S(1)}, bf16[128,128]{1,0:T(8,128)(2,1)}, u32[]{:S(2)}) copy-start(bf16[128,128]{1,0:T(8,128)(2,1)} %constant.32.clone.unit_ref) | copy-start | bytes 98308
  318.3 42.3 %copy-start.1 = (f32[128,8,8]{0,2,1:T(8,128)S(1)}, f32[128,8,8]{0,2,1:T(8,128)}, u32[]{:S(2)}) copy-start(f32[128,8,8]{0,2,1:T(8,128)} %param.16) | copy-start | bytes 98308

commit v2 on v1

v2 whole, which is shorter than its diff:
```python
import math

import jax
import jax.numpy as jnp
import numpy as np
from jax import lax
from jax.experimental import pallas as pl
from jax.experimental.pallas import tpu as pltpu
from jax.sharding import PartitionSpec as P

X = 240
Y = 128
NZ = 64
BE = 8
P_SIZE = 512
KB = 4
C = 64
PROJ = 8
XB = X // BE
PAIRS = XB // 2
NBAND = 16
NSLAB = 8
NDEV = NBAND * NSLAB
NGROUP = 16
ROWS = 2 * NDEV
HALF = 64
STEP = 3
PLANES = 4
KINETIC_SCALE = 8.0
AXES = ("band", "slab")
F32 = jnp.float32
BF16 = jnp.bfloat16
VMEM_LIMIT = 48 * 1024 * 1024


def cos_sin(length):
    counter = np.arange(length)
    phases = (counter[:, None] * counter[None, :] % length) * (2.0 * math.pi / length)
    return np.cos(phases) / math.sqrt(length), np.sin(phases) / math.sqrt(length)


def bf16_table(values):
    return jnp.asarray(np.asarray(values, np.float32), dtype=BF16)


def x_order():
    x = np.arange(X).reshape(XB, BE // 2, 2)
    return x.transpose(2, 0, 1).reshape(-1)


def point_order():
    q = np.arange(P_SIZE).reshape(BE, BE, BE)
    return q.transpose(1, 0, 2).reshape(-1)


def nt(a, b):
    return lax.dot_general(a, b, (((1,), (1,)), ((), ())), preferred_element_type=F32)


def nn(a, b):
    return lax.dot_general(a, b, (((1,), (0,)), ((), ())), preferred_element_type=F32)


def to_grid_kernel(spec_ref, ty_ref, tx_ref, out_ref, across_ref):
    for e in range(BE):
        plane = jnp.concatenate([spec_ref[0, 0, e], spec_ref[1, 0, e]], axis=1)
        across = nt(ty_ref[...], plane)
        across_ref[:, :, e] = across.reshape(2, NBAND, BE, X)
    low = lax.broadcasted_iota(jnp.int32, (X // 2, 128), 1) < HALF
    for c in range(0, NBAND, 2):
        re = [across_ref[0, c + i].reshape(BE * BE, X).astype(BF16) for i in range(2)]
        im = [across_ref[1, c + i].reshape(BE * BE, X).astype(BF16) for i in range(2)]
        whole = nt(tx_ref[0], jnp.concatenate([re[0], im[0], re[1], im[1]], axis=0)) + nt(
            tx_ref[1], jnp.concatenate([-im[0], re[0], -im[1], re[1]], axis=0)
        )
        for i in range(2):
            even = whole[: X // 2, i * 128 : (i + 1) * 128]
            odd = whole[X // 2 :, i * 128 : (i + 1) * 128]
            first = jnp.where(low, even, pltpu.roll(odd, HALF, 1))
            second = jnp.where(low, pltpu.roll(even, HALF, 1), odd)
            rows = jnp.stack(
                [first.reshape(PAIRS, 8, 128), second.reshape(PAIRS, 8, 128)], axis=1
            ).reshape(X, 128)
            out_ref[c + i, 0] = rows.astype(BF16)


def to_grid(orbitals):
    cy, sy = cos_sin(Y)
    ty = bf16_table(np.block([[cy, -sy], [sy, cy]]))
    cx, sx = cos_sin(X)
    order = x_order()
    tx = bf16_table(np.stack([cx[order], sx[order]]))
    return pl.pallas_call(
        to_grid_kernel,
        grid=(NSLAB,),
        in_specs=[
            pl.BlockSpec((2, 1, BE, X, Y), lambda s: (0, 0, s, 0, 0)),
            pl.BlockSpec((2 * Y, 2 * Y), lambda s: (0, 0)),
            pl.BlockSpec((2, X, X), lambda s: (0, 0, 0)),
        ],
        out_specs=pl.BlockSpec((NBAND, 1, X, 128), lambda s: (0, s, 0, 0)),
        out_shape=jax.ShapeDtypeStruct((NBAND, NSLAB, X, 128), BF16),
        scratch_shapes=[pltpu.VMEM((2, NBAND, BE, BE, X), F32)],
        compiler_params=pltpu.CompilerParams(vmem_limit_bytes=VMEM_LIMIT),
        name="to_grid",
    )(orbitals, ty, tx)


def turned_rows(bricks_ref, pair):
    turned = jnp.swapaxes(bricks_ref[:, pair * 16 : (pair + 1) * 16], 0, 1)
    return [
        jnp.concatenate(
            [
                jnp.concatenate([turned[part * 8 + low * 4 + high] for high in range(4)], axis=1)
                for part in range(2)
            ],
            axis=0,
        )
        for low in range(2)
    ]


def project_kernel(groups_ref, bricks_ref, proj_ref, sums_ref, coef_ref):
    t = pl.program_id(0)

    @pl.when(t == 0)
    def _():
        coef_ref[...] = jnp.zeros_like(coef_ref)

    for pair in range(STEP):
        rows = turned_rows(bricks_ref, pair)
        for low in range(2):
            b = 2 * pair + low
            partial = nt(proj_ref[b], rows[low])
            for k in range(KB):
                g = groups_ref[(2 * STEP * t + b) * KB + k]
                coef_ref[g] += partial[k * C : (k + 1) * C]

    @pl.when(t == PAIRS // STEP - 1)
    def _():
        sums_ref[...] = coef_ref[...].astype(BF16)


def project(groups, bricks, proj):
    return pl.pallas_call(
        project_kernel,
        grid_spec=pltpu.PrefetchScalarGridSpec(
            num_scalar_prefetch=1,
            grid=(PAIRS // STEP,),
            in_specs=[
                pl.BlockSpec((NDEV, 16 * STEP, 128), lambda t, g: (0, t, 0)),
                pl.BlockSpec((2 * STEP, KB * C, P_SIZE), lambda t, g: (t, 0, 0)),
            ],
            out_specs=pl.BlockSpec((NGROUP, C, ROWS), lambda t, g: (0, 0, 0)),
            scratch_shapes=[pltpu.VMEM((NGROUP, C, ROWS), F32)],
        ),
        out_shape=jax.ShapeDtypeStruct((NGROUP, C, ROWS), BF16),
        compiler_params=pltpu.CompilerParams(vmem_limit_bytes=VMEM_LIMIT),
        name="project",
    )(groups, bricks, proj)


def couple_kernel(sums_ref, strength_ref, out_ref):
    total = jnp.sum(sums_ref[...].astype(F32), axis=0)
    strength = 0.5 * (strength_ref[0] + strength_ref[0].T)
    scaled = strength[:, 0:1] * total[0:1]
    for j in range(1, PROJ):
        scaled = scaled + strength[:, j : j + 1] * total[j : j + 1]
    out_ref[...] = jnp.broadcast_to(scaled[None], (NDEV, PROJ, ROWS)).astype(BF16)


def couple(sums, strengths):
    return pl.pallas_call(
        couple_kernel,
        out_shape=jax.ShapeDtypeStruct((NDEV, PROJ, ROWS), BF16),
        compiler_params=pltpu.CompilerParams(vmem_limit_bytes=VMEM_LIMIT),
        name="couple",
    )(sums, strengths)


def act_kernel(groups_ref, coupled_ref, bricks_ref, proj_ref, pot_ref, out_ref, picks_ref):
    t = pl.program_id(0)

    @pl.when(t == 0)
    def _():
        unit = (
            lax.broadcasted_iota(jnp.int32, (ROWS, ROWS), 0)
            == lax.broadcasted_iota(jnp.int32, (ROWS, ROWS), 1)
        ).astype(BF16)
        zeros = jnp.zeros((C, ROWS), BF16)
        for g in range(NGROUP):
            block = coupled_ref[g]
            both = nt(unit, jnp.concatenate([block, zeros, zeros, block], axis=0)).astype(BF16)
            picks_ref[0, g] = both[:, : 2 * C]
            picks_ref[1, g] = both[:, 2 * C :]

    for pair in range(STEP):
        rows = turned_rows(bricks_ref, pair)
        pieces = [None] * 16
        for low in range(2):
            b = 2 * pair + low
            g = [groups_ref[(2 * STEP * t + b) * KB + k] for k in range(KB)]
            picked = jnp.concatenate(
                [picks_ref[0, g[0]] + picks_ref[1, g[1]], picks_ref[0, g[2]] + picks_ref[1, g[3]]],
                axis=1,
            )
            acted = nn(picked, proj_ref[b]) + pot_ref[b] * rows[low].astype(F32)
            acted = acted.astype(BF16)
            for part in range(2):
                for high in range(4):
                    pieces[part * 8 + low * 4 + high] = acted[
                        part * NDEV : (part + 1) * NDEV, high * 128 : (high + 1) * 128
                    ]
        out_ref[:, pair * 16 : (pair + 1) * 16] = jnp.swapaxes(jnp.stack(pieces), 0, 1)


def act(groups, coupled, bricks, proj, pot):
    return pl.pallas_call(
        act_kernel,
        grid_spec=pltpu.PrefetchScalarGridSpec(
            num_scalar_prefetch=1,
            grid=(PAIRS // STEP,),
            in_specs=[
                pl.BlockSpec((NGROUP, C, ROWS), lambda t, g: (0, 0, 0)),
                pl.BlockSpec((NDEV, 16 * STEP, 128), lambda t, g: (0, t, 0)),
                pl.BlockSpec((2 * STEP, KB * C, P_SIZE), lambda t, g: (t, 0, 0)),
                pl.BlockSpec((2 * STEP, 1, P_SIZE), lambda t, g: (t, 0, 0)),
            ],
            out_specs=pl.BlockSpec((NDEV, 16 * STEP, 128), lambda t, g: (0, t, 0)),
            scratch_shapes=[pltpu.VMEM((2, NGROUP, ROWS, 2 * C), BF16)],
        ),
        out_shape=jax.ShapeDtypeStruct((NDEV, X, 128), BF16),
        compiler_params=pltpu.CompilerParams(vmem_limit_bytes=VMEM_LIMIT),
        name="act",
    )(groups, coupled, bricks, proj, pot)


def to_waves_kernel(
    grid_ref, spec_ref, below_ref, above_ref, unit_ref, tx_ref, ty_ref, planar_ref, out_ref, turned_ref
):
    s = pl.program_id(0)

    for c in range(0, NBAND, 2):
        two = jnp.concatenate([grid_ref[c, 0], grid_ref[c + 1, 0]], axis=1)
        turned_ref[:, :, c : c + 2] = nt(unit_ref[...], two).reshape(2, BE, 2, BE, X)
    has_below = (s > 0).astype(F32)
    has_above = (s < NSLAB - 1).astype(F32)
    for first in range(0, BE, PLANES):
        even = turned_ref[0, first : first + PLANES].reshape(PLANES * Y, X).astype(BF16)
        odd = turned_ref[1, first : first + PLANES].reshape(PLANES * Y, X).astype(BF16)
        halves = nt(tx_ref[0], even) + nt(tx_ref[1], odd)
        for i in range(PLANES):
            e = first + i
            half = halves[:, i * Y : (i + 1) * Y]
            half = jnp.concatenate([half[:X], half[X:]], axis=1).astype(BF16)
            result = nn(half, ty_ref[...])
            for o in range(2):
                here = spec_ref[o, 0, e].astype(F32)
                if e == 0:
                    below = below_ref[o, 0, 0].astype(F32) * has_below
                else:
                    below = spec_ref[o, 0, e - 1].astype(F32)
                if e == BE - 1:
                    above = above_ref[o, 0, 0].astype(F32) * has_above
                else:
                    above = spec_ref[o, 0, e + 1].astype(F32)
                kinetic = planar_ref[...] * here + 0.5 * (2.0 * here - above - below)
                out_ref[o, 0, e] = (result[:, o * Y : (o + 1) * Y] + kinetic).astype(BF16)


def to_waves(grid, orbitals):
    cx, sx = cos_sin(X)
    x = np.arange(X).reshape(PAIRS, 2, BE // 2, 2)
    tables = []
    for low in range(2):
        own = x[..., low].reshape(PAIRS, 8)
        re, im = np.zeros((2 * X, PAIRS, 8)), np.zeros((2 * X, PAIRS, 8))
        re[:X], re[X:] = cx[:, own], -sx[:, own]
        im[:X], im[X:] = sx[:, own], cx[:, own]
        tables.append(np.stack([re, im], axis=2).reshape(2 * X, X))
    tx = bf16_table(np.stack(tables))
    spot = np.arange(256).reshape(2, 2, BE, BE).transpose(1, 2, 0, 3).reshape(-1)
    unit = bf16_table(np.eye(256)[spot])
    cy, sy = cos_sin(Y)
    ty = bf16_table(np.block([[cy, -sy], [sy, cy]]))
    wave_x = np.minimum(np.arange(X), X - np.arange(X)).astype(np.float32) / X
    wave_y = np.minimum(np.arange(Y), Y - np.arange(Y)).astype(np.float32) / Y
    planar = jnp.asarray(
        KINETIC_SCALE * (wave_x[:, None] * wave_x[:, None] + wave_y[None, :] * wave_y[None, :]), dtype=F32
    )
    return pl.pallas_call(
        to_waves_kernel,
        grid=(NSLAB,),
        in_specs=[
            pl.BlockSpec((NBAND, 1, X, 128), lambda s: (0, s, 0, 0)),
            pl.BlockSpec((2, 1, BE, X, Y), lambda s: (0, 0, s, 0, 0)),
            pl.BlockSpec((2, 1, 1, X, Y), lambda s: (0, 0, jnp.maximum(s * BE - 1, 0), 0, 0)),
            pl.BlockSpec((2, 1, 1, X, Y), lambda s: (0, 0, jnp.minimum(s * BE + BE, NZ - 1), 0, 0)),
            pl.BlockSpec((256, 256), lambda s: (0, 0)),
            pl.BlockSpec((2, 2 * X, X), lambda s: (0, 0, 0)),
            pl.BlockSpec((2 * Y, 2 * Y), lambda s: (0, 0)),
            pl.BlockSpec((X, Y), lambda s: (0, 0)),
        ],
        out_specs=pl.BlockSpec((2, 1, BE, X, Y), lambda s: (0, 0, s, 0, 0)),
        out_shape=jax.ShapeDtypeStruct((2, 1, NZ, X, Y), BF16),
        scratch_shapes=[pltpu.VMEM((2, BE, NBAND, BE, X), F32)],
        compiler_params=pltpu.CompilerParams(vmem_limit_bytes=VMEM_LIMIT),
        name="to_waves",
    )(grid, orbitals, orbitals, orbitals, unit, tx, ty, planar)


def exchange(array):
    return lax.all_to_all(array, AXES, split_axis=0, concat_axis=0, tiled=True)


def on_device(orbitals, potential, projector, block_group, strengths):
    groups = block_group.reshape(-1)
    order = point_order()
    turn = np.zeros((P_SIZE, P_SIZE), np.float32)
    turn[order, np.arange(P_SIZE)] = 1.0
    proj = nn(projector.reshape(XB * KB * C, P_SIZE), jnp.asarray(turn, dtype=BF16)).astype(BF16)
    proj = proj.reshape(XB, KB * C, P_SIZE)
    pot = potential.reshape(XB, BE, BE, BE).transpose(0, 2, 1, 3).reshape(XB, 1, P_SIZE)
    own = lax.axis_index(AXES)
    strength = lax.dynamic_slice_in_dim(strengths, own, 1, 0)

    bricks = exchange(to_grid(orbitals).reshape(NDEV, X, 128))
    sums = project(groups, bricks, proj)
    coupled = exchange(couple(exchange(sums.reshape(NDEV, PROJ, ROWS)), strength))
    acted = act(groups, coupled.reshape(NGROUP, C, ROWS), bricks, proj, pot)
    returned = exchange(acted).reshape(NBAND, NSLAB, X, 128)
    return to_waves(returned, orbitals)


def solution(mesh):
    in_specs = (
        P(None, AXES, None, None, None),
        P("slab", None, "band", None),
        P("slab", None, "band", None, None, None),
        P("slab", None, "band", None),
        P(),
    )
    out_specs = P(None, AXES, None, None, None)
    return jax.shard_map(
        on_device, mesh=mesh, in_specs=in_specs, out_specs=out_specs, check_vma=False
    )
```

time: 362 us -> 307 us (0.85)
  Pallas kernels: 110 us -> 55.7 us
    pallas_call x1, Pallas kernels: 42.3 us -> 17.3 us  [to_waves(): pl.pallas_call(to_waves_kernel, grid=(NSLAB,), in_specs=[pl.BlockSpec((NB...]
    pallas_call x1, Pallas kernels: 29.5 us -> 13.4 us  [to_grid(): pl.pallas_call(to_grid_kernel, grid=(NSLAB,), in_specs=[pl.BlockSpec((2,...]
    pallas_call x1, Pallas kernels: 19.1 us -> 9.89 us  [project(): pl.pallas_call(project_kernel, grid_spec=pltpu.PrefetchScalarGridSpec(num...]
    pallas_call x1, Pallas kernels: 18.3 us -> 14.1 us  [act(): pl.pallas_call(act_kernel, grid_spec=pltpu.PrefetchScalarGridSpec(num_sca...]
  transfers between devices with their start and end apart: 3 -> 3, of which waited for: 3 -> 3; matrix products, arithmetic and copies ran while one was open for 6% -> 7% of each run, Pallas kernels for 0% -> 0%
where the time goes in v2:
time: 307 us; the launch traced here: 306 us
  waiting for transfers between devices  99.7 us (32%)
  blocking collectives  98.5 us (32%)
  Pallas kernels  55.7 us (18%)
  starting transfers between devices  29.2 us (10%)
  local copies, waits for them, and re-layouts  13.1 us (4%)
  matrix products  9.81 us (3%)
    all_to_all x3, waiting for transfers between devices, exchange(): return lax.all_to_all(array, AXES, split_axis=0, concat_axis=0, tiled=True)  99.7 us
    all_to_all x1, blocking collectives, exchange(): return lax.all_to_all(array, AXES, split_axis=0, concat_axis=0, tiled=True)  98.5 us
    all_to_all x3, starting transfers between devices, exchange(): return lax.all_to_all(array, AXES, split_axis=0, concat_axis=0, tiled=True)  29.2 us
    pallas_call x1, Pallas kernels, to_waves(): pl.pallas_call(to_waves_kernel, grid=(NSLAB,), in_specs=[pl.BlockSpec((NB...  17.3 us
    pallas_call x1, Pallas kernels, act(): pl.pallas_call(act_kernel, grid_spec=pltpu.PrefetchScalarGridSpec(num_sca...  14.1 us
    pallas_call x1, Pallas kernels, to_grid(): pl.pallas_call(to_grid_kernel, grid=(NSLAB,), in_specs=[pl.BlockSpec((2,...  13.4 us
    convert_element_type x1, local copies, waits for them, and re-layouts, on_device(): nn(projector.reshape(XB * KB * C, P_SIZE), jnp.asarray(turn, dtype=BF16))  10.6 us
    pallas_call x1, Pallas kernels, project(): pl.pallas_call(project_kernel, grid_spec=pltpu.PrefetchScalarGridSpec(num...  9.89 us
  transfers between devices with their start and end apart: 3, of which 3 were waited for; matrix products, arithmetic and copies ran while one was open for 7% of the time, Pallas kernels for 0%

profile of v2, /device:TPU:1, one launch (start us, length us, event | category | flops | bytes accessed | tf_op | source)
XLA Modules:
  0.0 306.1 jit_solution(15422454216257649591)
XLA Ops:
  0.0 0.0 copy-start
  0.0 0.0 copy-start.2
  0.0 0.9 copy-done.2
  0.9 0.0 copy-start.5
  0.9 0.9 copy-done.5
  1.9 13.4 %to_grid.1 = bf16[16,8,240,128]{3,2,1,0:T(8,128)(2,1)} custom-call(bf16[2,1,64,240,128]{4,3,2,1,0:T(8,128)(2,1)} %above_ref.1, bf16[256,256]{1,0:T(8,128)(2,1)S(1)} %copy-done.2, bf16[2,240,240]{2,1,0:T(8,128)(2,1)S(1)} %copy-done.5), custom_call_target="tpu_custom_call" | custom-call | tf_op jit(solution)/shard_map/to_grid/pallas_call | solution.py:93
  15.3 0.0 copy-start.9
  15.3 0.0 copy-start.10
  15.3 11.9 %all-to-all-start = ((bf16[128,240,128]{2,1,0:T(8,128)(2,1)}), bf16[128,240,128]{2,1,0:T(8,128)(2,1)}, u32[]{:S(2)}, u32[]{:S(2)}) async-start(bf16[128,240,128]{2,1,0:T(8,128)(2,1)} %bitcast.20), calls=%async_computation | async-start | bytes 15728640 | tf_op jit(solution)/shard_map/all_to_all | solution.py:313
  27.2 0.0 copy-done.9
  27.2 0.1 copy.17
  27.3 0.1 reshape.27.groups_ref
  27.4 0.0 copy-done.10
  27.4 9.8 %fusion = bf16[7680,512]{0,1:T(8,128)(2,1)} fusion(bf16[512,512]{1,0:T(8,128)(2,1)S(1)} %copy-done.10, bf16[7680,512]{1,0:T(8,128)(2,1)} %bitcast.23), kind=kOutput, calls=%fused_computation.1 | convolution fusion | flops 4030464000 | bytes 16252928 | tf_op jit(solution)/shard_map/dot_general | solution.py:61
  37.2 10.6 %copy.18 = bf16[7680,512]{1,0:T(8,128)(2,1)} copy(bf16[7680,512]{0,1:T(8,128)(2,1)} %fusion) | data formatting | bytes 15728640 | tf_op jit(solution)/shard_map/convert_element_type | solution.py:321
  47.8 72.8 %all-to-all-done.bricks_ref = bf16[128,240,128]{2,1,0:T(8,128)(2,1)} async-done(((bf16[128,240,128]{2,1,0:T(8,128)(2,1)}), bf16[128,240,128]{2,1,0:T(8,128)(2,1)}, u32[]{:S(2)}, u32[]{:S(2)}) %all-to-all-start) | async-done | bytes 7864352 | tf_op jit(solution)/shard_map/all_to_all | solution.py:313
  120.6 0.0 copy-start.8
  120.6 9.9 %project.1 = bf16[16,64,256]{2,1,0:T(8,128)(2,1)} custom-call(s32[120]{0:T(128)S(1)} %reshape.27.groups_ref, bf16[128,240,128]{2,1,0:T(8,128)(2,1)} %all-to-all-done.bricks_ref, bf16[30,256,512]{2,1,0:T(8,128)(2,1)} %bitcast.17), custom_call_target="tpu_custom_call" | custom-call | tf_op jit(solution)/shard_map/project/pallas_call | solution.py:145
  130.5 12.7 %all-to-all-start.1 = ((bf16[128,8,256]{2,1,0:T(8,128)(2,1)}), bf16[128,8,256]{2,1,0:T(8,128)(2,1)S(1)}, u32[]{:S(2)}, u32[]{:S(2)}) async-start(bf16[128,8,256]{2,1,0:T(8,128)(2,1)} %bitcast.4), calls=%async_computation.1 | async-start | bytes 1048576 | tf_op jit(solution)/shard_map/all_to_all | solution.py:313
  143.1 0.0 copy-done
  143.2 0.1 constant_dynamic-slice_fusion
  143.2 0.1 copy.23.strength_ref
  143.3 13.5 %all-to-all-done.1.sums_ref = bf16[128,8,256]{2,1,0:T(8,128)(2,1)S(1)} async-done(((bf16[128,8,256]{2,1,0:T(8,128)(2,1)}), bf16[128,8,256]{2,1,0:T(8,128)(2,1)S(1)}, u32[]{:S(2)}, u32[]{:S(2)}) %all-to-all-start.1) | async-done | bytes 524320 | tf_op jit(solution)/shard_map/all_to_all | solution.py:313
  156.8 1.0 couple.1
  157.8 4.6 %all-to-all-start.2 = ((bf16[128,8,256]{2,1,0:T(8,128)(2,1)}), bf16[128,8,256]{2,1,0:T(8,128)(2,1)S(1)}, u32[]{:S(2)}, u32[]{:S(2)}) async-start(bf16[128,8,256]{2,1,0:T(8,128)(2,1)} %couple.1), calls=%async_computation.2 | async-start | bytes 1048576 | tf_op jit(solution)/shard_map/all_to_all | solution.py:313
  162.4 0.0 copy-done.8
  162.4 0.1 copy.20
  162.6 0.1 copy.22.pot_ref
  162.7 13.5 %all-to-all-done.2 = bf16[128,8,256]{2,1,0:T(8,128)(2,1)S(1)} async-done(((bf16[128,8,256]{2,1,0:T(8,128)(2,1)}), bf16[128,8,256]{2,1,0:T(8,128)(2,1)S(1)}, u32[]{:S(2)}, u32[]{:S(2)}) %all-to-all-start.2) | async-done | bytes 524320 | tf_op jit(solution)/shard_map/all_to_all | solution.py:313
  176.2 14.1 %act.1 = bf16[128,240,128]{2,1,0:T(8,128)(2,1)} custom-call(s32[120]{0:T(128)S(1)} %reshape.27.groups_ref, bf16[16,64,256]{2,1,0:T(8,128)(2,1)S(1)} %bitcast.16, bf16[128,240,128]{2,1,0:T(8,128)(2,1)} %all-to-all-done.bricks_ref, bf16[30,256,512]{2,1,0:T(8,128)(2,1)} %bitcast.18, f32[30,1,512]{2,1,0:T(1,128)S(1)} %copy.22.pot_ref), custom_call_target="tpu_custom_call" | custom-call | tf_op jit(solution)/shard_map/act/pallas_call | solution.py:218
  190.3 0.0 copy-start.3
  190.3 0.0 copy-start.4
  190.3 0.0 copy-start.6
  190.3 0.0 copy-start.7
  190.3 98.5 %all_to_all.20 = bf16[128,240,128]{2,1,0:T(8,128)(2,1)} all-to-all(bf16[128,240,128]{2,1,0:T(8,128)(2,1)} %act.1), channel_id=1, replica_groups=mesh['band'=16,'slab'=8] {'band','slab'}, dimensions={0} | all-to-all | bytes 15728640 | tf_op jit(solution)/shard_map/all_to_all | solution.py:313
  288.8 0.0 copy-done.3
  288.8 0.0 copy-done.4
  288.8 0.0 copy-done.6
  288.8 0.0 copy-done.7
  288.8 0.0 copy-start.1
  288.8 17.3 %to_waves.1 = bf16[2,1,64,240,128]{4,3,2,1,0:T(8,128)(2,1)} custom-call(bf16[16,8,240,128]{3,2,1,0:T(8,128)(2,1)} %bitcast.19, bf16[2,1,64,240,128]{4,3,2,1,0:T(8,128)(2,1)} %above_ref.1, bf16[2,1,64,240,128]{4,3,2,1,0:T(8,128)(2,1)} %above_ref.1, bf16[2,1,64,240,128]{4,3,2,1,0:T(8,128)(2,1)} %above_ref.1, bf16[256,256]{1,0:T(8,128)(2,1)S(1)} %copy-done.6, ...), custom_call_target="tpu_custom_call" | custom-call | tf_op jit(solution)/shard_map/to_waves/pallas_call | solution.py:291
  306.1 0.0 copy-done.1
  (1 shorter events, 0.0 us)
Async XLA Ops:
  0.0 143.1 %copy-start = (f32[128,8,8]{0,2,1:T(8,128)S(1)}, f32[128,8,8]{0,2,1:T(8,128)}, u32[]{:S(2)}) copy-start(f32[128,8,8]{0,2,1:T(8,128)} %param.16) | copy-start | bytes 98308
  0.0 0.9 copy-start.2
  0.9 0.9 copy-start.5
  15.3 11.9 %copy-start.9 = (s32[1,30,1,4]{1,3,2,0:T(4,128)S(1)}, s32[1,30,1,4]{1,3,2,0:T(4,128)}, u32[]{:S(2)}) copy-start(s32[1,30,1,4]{1,3,2,0:T(4,128)} %param.15) | copy-start | bytes 1444
  15.3 12.1 %copy-start.10 = (bf16[512,512]{1,0:T(8,128)(2,1)S(1)}, bf16[512,512]{1,0:T(8,128)(2,1)}, u32[]{:S(2)}) copy-start(bf16[512,512]{1,0:T(8,128)(2,1)} %constant.27.clone) | copy-start | bytes 1572868
  15.3 105.3 %all-to-all-start = ((bf16[128,240,128]{2,1,0:T(8,128)(2,1)}), bf16[128,240,128]{2,1,0:T(8,128)(2,1)}, u32[]{:S(2)}, u32[]{:S(2)}) async-start(bf16[128,240,128]{2,1,0:T(8,128)(2,1)} %bitcast.20), calls=%async_computation | async-start | bytes 15728640 | tf_op jit(solution)/shard_map/all_to_all | solution.py:313
  120.6 41.9 %copy-start.8 = (f32[1,30,1,512]{3,2,1,0:T(1,128)S(1)}, f32[1,30,1,512]{3,2,1,0:T(1,128)}, u32[]{:S(2)}) copy-start(f32[1,30,1,512]{3,2,1,0:T(1,128)} %param.13) | copy-start | bytes 184324
  130.5 26.3 %all-to-all-start.1 = ((bf16[128,8,256]{2,1,0:T(8,128)(2,1)}), bf16[128,8,256]{2,1,0:T(8,128)(2,1)S(1)}, u32[]{:S(2)}, u32[]{:S(2)}) async-start(bf16[128,8,256]{2,1,0:T(8,128)(2,1)} %bitcast.4), calls=%async_computation.1 | async-start | bytes 1048576 | tf_op jit(solution)/shard_map/all_to_all | solution.py:313
  157.8 18.4 %all-to-all-start.2 = ((bf16[128,8,256]{2,1,0:T(8,128)(2,1)}), bf16[128,8,256]{2,1,0:T(8,128)(2,1)S(1)}, u32[]{:S(2)}, u32[]{:S(2)}) async-start(bf16[128,8,256]{2,1,0:T(8,128)(2,1)} %couple.1), calls=%async_computation.2 | async-start | bytes 1048576 | tf_op jit(solution)/shard_map/all_to_all | solution.py:313
  190.3 98.5 %copy-start.3 = (bf16[256,256]{1,0:T(8,128)(2,1)S(1)}, bf16[256,256]{1,0:T(8,128)(2,1)}, u32[]{:S(2)}) copy-start(bf16[256,256]{1,0:T(8,128)(2,1)} %constant.28.clone.ty_ref) | copy-start | bytes 393220
  190.3 98.5 %copy-start.4 = (bf16[2,480,240]{2,1,0:T(8,128)(2,1)S(1)}, bf16[2,480,240]{2,1,0:T(8,128)(2,1)}, u32[]{:S(2)}) copy-start(bf16[2,480,240]{2,1,0:T(8,128)(2,1)} %constant.30.clone.tx_ref) | copy-start | bytes 1382404
  190.3 98.5 %copy-start.6 = (bf16[256,256]{1,0:T(8,128)(2,1)S(1)}, bf16[256,256]{1,0:T(8,128)(2,1)}, u32[]{:S(2)}) copy-start(bf16[256,256]{1,0:T(8,128)(2,1)} %constant.31.clone.unit_ref) | copy-start | bytes 393220
  190.3 98.5 %copy-start.7 = (f32[240,128]{1,0:T(8,128)S(1)}, f32[240,128]{1,0:T(8,128)}, u32[]{:S(2)}) copy-start(f32[240,128]{1,0:T(8,128)} %constant.32.clone.planar_ref) | copy-start | bytes 368644
  288.8 17.4 %copy-start.1 = (f32[128,8,8]{0,2,1:T(8,128)S(1)}, f32[128,8,8]{0,2,1:T(8,128)}, u32[]{:S(2)}) copy-start(f32[128,8,8]{0,2,1:T(8,128)} %param.16) | copy-start | bytes 98308

commit v3 on v2

v3 whole, which is shorter than its diff:
```python
import math
from itertools import zip_longest

import jax
import jax.numpy as jnp
import numpy as np
from jax import lax
from jax.experimental import pallas as pl
from jax.experimental.pallas import tpu as pltpu
from jax.sharding import PartitionSpec as P

X = 240
Y = 128
NZ = 64
BE = 8
HX = X // 2
P_SIZE = 512
KB = 4
C = 64
PROJ = 8
XB = X // BE
PAIRS = XB // 2
NBAND = 16
NSLAB = 8
NDEV = NBAND * NSLAB
NGROUP = 16
ROWS = 2 * NDEV
HALF = 64
STEP = 3
PROJECT_STEP = 5
PLANES = 4
KINETIC_SCALE = 8.0
AXES = ("band", "slab")
ORDER = ("slab", "band")
F32 = jnp.float32
BF16 = jnp.bfloat16
MIB = 1024 * 1024


def cos_sin(length):
    counter = np.arange(length)
    phases = (counter[:, None] * counter[None, :] % length) * (2.0 * math.pi / length)
    return np.cos(phases) / math.sqrt(length), np.sin(phases) / math.sqrt(length)


def bf16_table(values):
    return jnp.asarray(np.asarray(values, np.float32), dtype=BF16)


def x_order():
    x = np.arange(X).reshape(XB, BE // 2, 2)
    return x.transpose(2, 0, 1).reshape(-1)


def point_order():
    q = np.arange(P_SIZE).reshape(BE, BE, BE)
    return q.transpose(1, 0, 2).reshape(-1)


def nt(a, b):
    return lax.dot_general(a, b, (((1,), (1,)), ((), ())), preferred_element_type=F32)


def nn(a, b):
    return lax.dot_general(a, b, (((1,), (0,)), ((), ())), preferred_element_type=F32)


def two_stages(t, first, second, slots):
    def beside(now, before):
        one = first(now) if now is not None else ()
        two = second(before) if before is not None else ()
        for _ in zip_longest(one, two):
            pass

    pl.when(t == 0)(lambda: beside(slots[0], None))
    pl.when((t > 0) & (t < NSLAB) & (t % 2 == 0))(lambda: beside(slots[0], slots[1]))
    pl.when((t < NSLAB) & (t % 2 == 1))(lambda: beside(slots[1], slots[0]))
    pl.when(t == NSLAB)(lambda: beside(None, slots[(NSLAB - 1) % 2]))


def ahead(t):
    return jnp.minimum(t, NSLAB - 1)


def behind(t):
    return jnp.maximum(t - 1, 0)


def to_grid_kernel(spec_ref, ty_ref, tx_ref, out_ref, *slots):
    def along_y(across_ref):
        for e in range(0, BE, 2):
            across = []
            for i in range(2):
                plane = jnp.concatenate([spec_ref[0, 0, e + i], spec_ref[1, 0, e + i]], axis=1)
                across.append(nt(ty_ref[...], plane))
                if i == 0:
                    yield
            across = jnp.stack([a.reshape(2, NBAND, BE, X) for a in across], axis=2)
            across_ref[:, :, e // 2] = across.reshape(2, NBAND, 2 * BE, X).astype(BF16)
            yield

    def along_x(across_ref):
        low = lax.broadcasted_iota(jnp.int32, (X // 2, 128), 1) < HALF
        for c in range(0, NBAND, 2):
            re = [across_ref[0, c + i].reshape(BE * BE, X) for i in range(2)]
            im = [across_ref[1, c + i].reshape(BE * BE, X) for i in range(2)]
            whole = nt(tx_ref[0], jnp.concatenate([re[0], im[0], re[1], im[1]], axis=0)) + nt(
                tx_ref[1], jnp.concatenate([-im[0], re[0], -im[1], re[1]], axis=0)
            )
            for i in range(2):
                even = whole[: X // 2, i * 128 : (i + 1) * 128]
                odd = whole[X // 2 :, i * 128 : (i + 1) * 128]
                first = jnp.where(low, even, pltpu.roll(odd, HALF, 1))
                second = jnp.where(low, pltpu.roll(even, HALF, 1), odd)
                rows = jnp.stack(
                    [first.reshape(PAIRS, 8, 128), second.reshape(PAIRS, 8, 128)], axis=1
                ).reshape(X, 128)
                out_ref[0, c + i] = rows.astype(BF16)
            yield

    two_stages(pl.program_id(0), along_y, along_x, slots)


def to_grid(orbitals):
    cy, sy = cos_sin(Y)
    ty = bf16_table(np.block([[cy, -sy], [sy, cy]]))
    cx, sx = cos_sin(X)
    order = x_order()
    tx = bf16_table(np.stack([cx[order], sx[order]]))
    return pl.pallas_call(
        to_grid_kernel,
        grid=(NSLAB + 1,),
        in_specs=[
            pl.BlockSpec((2, 1, BE, X, Y), lambda t: (0, 0, ahead(t), 0, 0)),
            pl.BlockSpec((2 * Y, 2 * Y), lambda t: (0, 0)),
            pl.BlockSpec((2, X, X), lambda t: (0, 0, 0)),
        ],
        out_specs=pl.BlockSpec((1, NBAND, X, 128), lambda t: (behind(t), 0, 0, 0)),
        out_shape=jax.ShapeDtypeStruct((NSLAB, NBAND, X, 128), BF16),
        scratch_shapes=[pltpu.VMEM((2, NBAND, BE // 2, 2 * BE, X), BF16)] * 2,
        compiler_params=pltpu.CompilerParams(vmem_limit_bytes=60 * MIB),
        name="to_grid",
    )(orbitals, ty, tx)


def turned_rows(bricks_ref, pair):
    turned = jnp.swapaxes(bricks_ref[:, pair * 16 : (pair + 1) * 16], 0, 1)
    return [
        jnp.concatenate(
            [
                jnp.concatenate([turned[part * 8 + low * 4 + high] for high in range(4)], axis=1)
                for part in range(2)
            ],
            axis=0,
        )
        for low in range(2)
    ]


def project_kernel(groups_ref, bricks_ref, proj_ref, sums_ref, coef_ref):
    t = pl.program_id(0)

    @pl.when(t == 0)
    def _():
        coef_ref[...] = jnp.zeros_like(coef_ref)

    for pair in range(PROJECT_STEP):
        rows = turned_rows(bricks_ref, pair)
        for low in range(2):
            b = 2 * pair + low
            partial = nt(proj_ref[b], rows[low])
            for k in range(KB):
                g = groups_ref[(2 * PROJECT_STEP * t + b) * KB + k]
                coef_ref[g] += partial[k * C : (k + 1) * C]

    @pl.when(t == PAIRS // PROJECT_STEP - 1)
    def _():
        sums_ref[...] = coef_ref[...].astype(BF16)


def project(groups, bricks, proj):
    return pl.pallas_call(
        project_kernel,
        grid_spec=pltpu.PrefetchScalarGridSpec(
            num_scalar_prefetch=1,
            grid=(PAIRS // PROJECT_STEP,),
            in_specs=[
                pl.BlockSpec((NDEV, 16 * PROJECT_STEP, 128), lambda t, g: (0, t, 0)),
                pl.BlockSpec((2 * PROJECT_STEP, KB * C, P_SIZE), lambda t, g: (t, 0, 0)),
            ],
            out_specs=pl.BlockSpec((NGROUP, C, ROWS), lambda t, g: (0, 0, 0)),
            scratch_shapes=[pltpu.VMEM((NGROUP, C, ROWS), F32)],
        ),
        out_shape=jax.ShapeDtypeStruct((NGROUP, C, ROWS), BF16),
        compiler_params=pltpu.CompilerParams(vmem_limit_bytes=60 * MIB),
        name="project",
    )(groups, bricks, proj)


def couple_kernel(sums_ref, strength_ref, out_ref):
    total = jnp.sum(sums_ref[...].astype(F32), axis=0)
    strength = 0.5 * (strength_ref[0] + strength_ref[0].T)
    scaled = strength[:, 0:1] * total[0:1]
    for j in range(1, PROJ):
        scaled = scaled + strength[:, j : j + 1] * total[j : j + 1]
    out_ref[...] = jnp.broadcast_to(scaled[None], (NDEV, PROJ, ROWS)).astype(BF16)


def couple(sums, strengths):
    return pl.pallas_call(
        couple_kernel,
        out_shape=jax.ShapeDtypeStruct((NDEV, PROJ, ROWS), BF16),
        compiler_params=pltpu.CompilerParams(vmem_limit_bytes=8 * MIB),
        name="couple",
    )(sums, strengths)


def act_kernel(groups_ref, coupled_ref, bricks_ref, proj_ref, pot_ref, out_ref, picks_ref):
    t = pl.program_id(0)

    @pl.when(t == 0)
    def _():
        unit = (
            lax.broadcasted_iota(jnp.int32, (ROWS, ROWS), 0)
            == lax.broadcasted_iota(jnp.int32, (ROWS, ROWS), 1)
        ).astype(BF16)
        zeros = jnp.zeros((C, ROWS), BF16)
        for g in range(NGROUP):
            block = coupled_ref[g]
            both = nt(unit, jnp.concatenate([block, zeros, zeros, block], axis=0)).astype(BF16)
            picks_ref[0, g] = both[:, : 2 * C]
            picks_ref[1, g] = both[:, 2 * C :]

    for pair in range(STEP):
        rows = turned_rows(bricks_ref, pair)
        pieces = [None] * 16
        for low in range(2):
            b = 2 * pair + low
            g = [groups_ref[(2 * STEP * t + b) * KB + k] for k in range(KB)]
            picked = jnp.concatenate(
                [picks_ref[0, g[0]] + picks_ref[1, g[1]], picks_ref[0, g[2]] + picks_ref[1, g[3]]],
                axis=1,
            )
            acted = nn(picked, proj_ref[b]) + pot_ref[b] * rows[low].astype(F32)
            acted = acted.astype(BF16)
            for part in range(2):
                for high in range(4):
                    pieces[part * 8 + low * 4 + high] = acted[
                        part * NDEV : (part + 1) * NDEV, high * 128 : (high + 1) * 128
                    ]
        out_ref[:, pair * 16 : (pair + 1) * 16] = jnp.swapaxes(jnp.stack(pieces), 0, 1)


def act(groups, coupled, bricks, proj, pot):
    return pl.pallas_call(
        act_kernel,
        grid_spec=pltpu.PrefetchScalarGridSpec(
            num_scalar_prefetch=1,
            grid=(PAIRS // STEP,),
            in_specs=[
                pl.BlockSpec((NGROUP, C, ROWS), lambda t, g: (0, 0, 0)),
                pl.BlockSpec((NDEV, 16 * STEP, 128), lambda t, g: (0, t, 0)),
                pl.BlockSpec((2 * STEP, KB * C, P_SIZE), lambda t, g: (t, 0, 0)),
                pl.BlockSpec((2 * STEP, 1, P_SIZE), lambda t, g: (t, 0, 0)),
            ],
            out_specs=pl.BlockSpec((NDEV, 16 * STEP, 128), lambda t, g: (0, t, 0)),
            scratch_shapes=[pltpu.VMEM((2, NGROUP, ROWS, 2 * C), BF16)],
        ),
        out_shape=pltpu.VMEM((NDEV, X, 128), BF16),
        compiler_params=pltpu.CompilerParams(vmem_limit_bytes=48 * MIB),
        name="act",
    )(groups, coupled, bricks, proj, pot)


def to_waves_kernel(
    grid_ref, spec_ref, below_ref, above_ref, tx_ref, ty_ref, planar_ref, out_ref, *slots
):
    t = pl.program_id(0)
    has_below = (t > 1).astype(F32)
    has_above = (t < NSLAB).astype(F32)

    def turn(turned_ref):
        for c in range(0, NBAND, 2):
            turned = [grid_ref[0, c + i].T.astype(F32).reshape(2, BE, 1, BE, X) for i in range(2)]
            turned = jnp.concatenate(turned, axis=2).reshape(2, BE, 2 * BE, X)
            turned_ref[:, :, c // 2] = turned.astype(BF16)
            yield

    def apply(turned_ref):
        for first in range(0, BE, PLANES):
            even = turned_ref[0, first : first + PLANES].reshape(PLANES * Y, X)
            odd = turned_ref[1, first : first + PLANES].reshape(PLANES * Y, X)
            even, odd = nt(tx_ref[0], even), nt(tx_ref[1], odd)
            front, back = even + odd, even - odd
            for i in range(PLANES):
                e = first + i
                cols = slice(i * Y, (i + 1) * Y)
                half = [
                    jnp.concatenate([front[o * HX : (o + 1) * HX, cols], back[o * HX : (o + 1) * HX, cols]], axis=0)
                    for o in range(2)
                ]
                half = jnp.concatenate(half, axis=1).astype(BF16)
                result = nn(half, ty_ref[...])
                for o in range(2):
                    here = spec_ref[o, 0, e].astype(F32)
                    if e == 0:
                        below = below_ref[o, 0, 0].astype(F32) * has_below
                    else:
                        below = spec_ref[o, 0, e - 1].astype(F32)
                    if e == BE - 1:
                        above = above_ref[o, 0, 0].astype(F32) * has_above
                    else:
                        above = spec_ref[o, 0, e + 1].astype(F32)
                    kinetic = planar_ref[...] * here - 0.5 * (above + below)
                    out_ref[o, 0, e] = (result[:, o * Y : (o + 1) * Y] + kinetic).astype(BF16)
                yield

    two_stages(t, turn, apply, slots)


def to_waves(grid, orbitals):
    cx, sx = cos_sin(X)
    x = np.arange(X).reshape(PAIRS, 2, BE // 2, 2)
    tables = []
    for low in range(2):
        own = x[..., low].reshape(PAIRS, 8)
        cos, sin = cx[:HX, own], sx[:HX, own]
        re, im = np.concatenate([cos, -sin]), np.concatenate([sin, cos])
        tables.append(np.stack([re, im], axis=2).reshape(X, X))
    tx = bf16_table(np.stack(tables))
    cy, sy = cos_sin(Y)
    ty = bf16_table(np.block([[cy, -sy], [sy, cy]]))
    wave_x = np.minimum(np.arange(X), X - np.arange(X)).astype(np.float32) / X
    wave_y = np.minimum(np.arange(Y), Y - np.arange(Y)).astype(np.float32) / Y
    planar = jnp.asarray(
        KINETIC_SCALE * (wave_x[:, None] * wave_x[:, None] + wave_y[None, :] * wave_y[None, :]) + 1.0, dtype=F32
    )
    return pl.pallas_call(
        to_waves_kernel,
        grid=(NSLAB + 1,),
        in_specs=[
            pl.BlockSpec((1, NBAND, X, 128), lambda t: (ahead(t), 0, 0, 0)),
            pl.BlockSpec((2, 1, BE, X, Y), lambda t: (0, 0, behind(t), 0, 0)),
            pl.BlockSpec((2, 1, 1, X, Y), lambda t: (0, 0, jnp.maximum(behind(t) * BE - 1, 0), 0, 0)),
            pl.BlockSpec((2, 1, 1, X, Y), lambda t: (0, 0, jnp.minimum(behind(t) * BE + BE, NZ - 1), 0, 0)),
            pl.BlockSpec((2, X, X), lambda t: (0, 0, 0)),
            pl.BlockSpec((2 * Y, 2 * Y), lambda t: (0, 0)),
            pl.BlockSpec((X, Y), lambda t: (0, 0)),
        ],
        out_specs=pl.BlockSpec((2, 1, BE, X, Y), lambda t: (0, 0, behind(t), 0, 0)),
        out_shape=jax.ShapeDtypeStruct((2, 1, NZ, X, Y), BF16),
        scratch_shapes=[pltpu.VMEM((2, BE, NBAND // 2, 2 * BE, X), BF16)] * 2,
        compiler_params=pltpu.CompilerParams(vmem_limit_bytes=48 * MIB),
        name="to_waves",
    )(grid, orbitals, orbitals, orbitals, tx, ty, planar)


def exchange(array):
    return lax.all_to_all(array, ORDER, split_axis=0, concat_axis=0, tiled=True)


def on_device(orbitals, potential, projector, block_group, strengths):
    groups = block_group.reshape(-1)
    order = point_order()
    turn = np.zeros((P_SIZE, P_SIZE), np.float32)
    turn[order, np.arange(P_SIZE)] = 1.0
    proj = nn(projector.reshape(XB * KB * C, P_SIZE), jnp.asarray(turn, dtype=BF16)).astype(BF16)
    proj = proj.reshape(XB, KB * C, P_SIZE)
    pot = potential.reshape(XB, BE, BE, BE).transpose(0, 2, 1, 3).reshape(XB, 1, P_SIZE)
    own = lax.axis_index(ORDER)
    strength = lax.dynamic_slice_in_dim(strengths, own, 1, 0)

    bricks = exchange(to_grid(orbitals).reshape(NDEV, X, 128))
    sums = project(groups, bricks, proj)
    coupled = exchange(couple(exchange(sums.reshape(NDEV, PROJ, ROWS)), strength))
    acted = act(groups, coupled.reshape(NGROUP, C, ROWS), bricks, proj, pot)
    returned = exchange(acted).reshape(NSLAB, NBAND, X, 128)
    return to_waves(returned, orbitals)


def solution(mesh):
    in_specs = (
        P(None, AXES, None, None, None),
        P("slab", None, "band", None),
        P("slab", None, "band", None, None, None),
        P("slab", None, "band", None),
        P(),
    )
    out_specs = P(None, AXES, None, None, None)
    return jax.shard_map(
        on_device, mesh=mesh, in_specs=in_specs, out_specs=out_specs, check_vma=False
    )
```

time: 307 us -> 296 us (0.964)
  Pallas kernels: 55.7 us -> 50 us
  starting transfers between devices: 29.2 us -> 25.2 us
    all_to_all x3, starting transfers between devices: 29.2 us -> 25.2 us  [exchange(): return lax.all_to_all(array, ORDER, split_axis=0, concat_axis=0, tiled=True)]
    pallas_call x2, Pallas kernels: 30.7 us -> 27.2 us  [the longest x1 14.4 us: to_waves(): pl.pallas_call(to_waves_kernel, grid=(NSLAB + 1,), in_specs=[pl.BlockSpec...]
  transfers between devices with their start and end apart: 3 -> 3, of which waited for: 3 -> 3; matrix products, arithmetic and copies ran while one was open for 7% -> 8% of each run, Pallas kernels for 0% -> 0%
where the time goes in v3:
time: 296 us; the launch traced here: 295 us
  waiting for transfers between devices  99.2 us (34%)
  blocking collectives  97.4 us (33%)
  Pallas kernels  50 us (17%)
  starting transfers between devices  25.2 us (9%)
  local copies, waits for them, and re-layouts  13.2 us (4%)
  matrix products  9.77 us (3%)
    all_to_all x3, waiting for transfers between devices, exchange(): return lax.all_to_all(array, ORDER, split_axis=0, concat_axis=0, tiled=True)  99.2 us
    all_to_all x1, blocking collectives, exchange(): return lax.all_to_all(array, ORDER, split_axis=0, concat_axis=0, tiled=True)  97.4 us
    all_to_all x3, starting transfers between devices, exchange(): return lax.all_to_all(array, ORDER, split_axis=0, concat_axis=0, tiled=True)  25.2 us
    pallas_call x1, Pallas kernels, to_waves(): pl.pallas_call(to_waves_kernel, grid=(NSLAB + 1,), in_specs=[pl.BlockSpec...  14.4 us
    pallas_call x1, Pallas kernels, to_grid(): pl.pallas_call(to_grid_kernel, grid=(NSLAB + 1,), in_specs=[pl.BlockSpec(...  12.8 us
    pallas_call x1, Pallas kernels, act(): pl.pallas_call(act_kernel, grid_spec=pltpu.PrefetchScalarGridSpec(num_sca...  12.2 us
    convert_element_type x1, local copies, waits for them, and re-layouts, on_device(): nn(projector.reshape(XB * KB * C, P_SIZE), jnp.asarray(turn, dtype=BF16))  10.5 us
    dot_general x1, matrix products, nn(): lax.dot_general(a, b, (((1,), (0,)), ((), ())), preferred_element_type=F32)  9.77 us
  transfers between devices with their start and end apart: 3, of which 3 were waited for; matrix products, arithmetic and copies ran while one was open for 8% of the time, Pallas kernels for 0%

profile of v3, /device:TPU:1, one launch (start us, length us, event | category | flops | bytes accessed | tf_op | source)
XLA Modules:
  0.0 294.8 jit_solution(6331804141845011782)
XLA Ops:
  0.0 0.0 copy-start
  0.0 12.8 %to_grid.1 = bf16[8,16,240,128]{3,2,1,0:T(8,128)(2,1)} custom-call(bf16[2,1,64,240,128]{4,3,2,1,0:T(8,128)(2,1)} %above_ref.1, bf16[256,256]{1,0:T(8,128)(2,1)} %constant.26.clone.ty_ref, bf16[2,240,240]{2,1,0:T(8,128)(2,1)} %constant.27.clone.tx_ref), custom_call_target="tpu_custom_call" | custom-call | tf_op jit(solution)/shard_map/to_grid/pallas_call | solution.py:130
  12.8 0.0 copy-start.7
  12.8 0.0 copy-start.8
  12.8 11.9 %all-to-all-start = ((bf16[128,240,128]{2,1,0:T(8,128)(2,1)}), bf16[128,240,128]{2,1,0:T(8,128)(2,1)}, u32[]{:S(2)}, u32[]{:S(2)}) async-start(bf16[128,240,128]{2,1,0:T(8,128)(2,1)} %bitcast.19), calls=%async_computation | async-start | bytes 15728640 | tf_op jit(solution)/shard_map/all_to_all | solution.py:359
  24.7 0.0 copy-done.7
  24.7 0.1 copy.16
  24.8 0.7 reshape.27.groups_ref
  25.5 0.0 copy-done.8
  25.5 9.8 %fusion = bf16[7680,512]{0,1:T(8,128)(2,1)} fusion(bf16[512,512]{1,0:T(8,128)(2,1)S(1)} %copy-done.8, bf16[7680,512]{1,0:T(8,128)(2,1)} %bitcast.24), kind=kOutput, calls=%fused_computation.1 | convolution fusion | flops 4030464000 | bytes 16252928 | tf_op jit(solution)/shard_map/dot_general | solution.py:65
  35.3 10.5 %copy.17 = bf16[7680,512]{1,0:T(8,128)(2,1)} copy(bf16[7680,512]{0,1:T(8,128)(2,1)} %fusion) | data formatting | bytes 15728640 | tf_op jit(solution)/shard_map/convert_element_type | solution.py:367
  45.8 73.5 %all-to-all-done.bricks_ref = bf16[128,240,128]{2,1,0:T(8,128)(2,1)} async-done(((bf16[128,240,128]{2,1,0:T(8,128)(2,1)}), bf16[128,240,128]{2,1,0:T(8,128)(2,1)}, u32[]{:S(2)}, u32[]{:S(2)}) %all-to-all-start) | async-done | bytes 7864352 | tf_op jit(solution)/shard_map/all_to_all | solution.py:359
  119.3 0.0 copy-start.6
  119.3 9.5 %project.1 = bf16[16,64,256]{2,1,0:T(8,128)(2,1)} custom-call(s32[120]{0:T(128)} %reshape.27.groups_ref, bf16[128,240,128]{2,1,0:T(8,128)(2,1)} %all-to-all-done.bricks_ref, bf16[30,256,512]{2,1,0:T(8,128)(2,1)} %bitcast.16), custom_call_target="tpu_custom_call" | custom-call | tf_op jit(solution)/shard_map/project/pallas_call | solution.py:182
  128.8 8.5 %all-to-all-start.1 = ((bf16[128,8,256]{2,1,0:T(8,128)(2,1)}), bf16[128,8,256]{2,1,0:T(8,128)(2,1)S(1)}, u32[]{:S(2)}, u32[]{:S(2)}) async-start(bf16[128,8,256]{2,1,0:T(8,128)(2,1)} %bitcast.20), calls=%async_computation.1 | async-start | bytes 1048576 | tf_op jit(solution)/shard_map/all_to_all | solution.py:359
  137.4 0.0 copy-done
  137.4 0.1 constant_dynamic-slice_fusion
  137.5 0.1 copy.22.strength_ref
  137.6 13.1 %all-to-all-done.1.sums_ref = bf16[128,8,256]{2,1,0:T(8,128)(2,1)S(1)} async-done(((bf16[128,8,256]{2,1,0:T(8,128)(2,1)}), bf16[128,8,256]{2,1,0:T(8,128)(2,1)S(1)}, u32[]{:S(2)}, u32[]{:S(2)}) %all-to-all-start.1) | async-done | bytes 524320 | tf_op jit(solution)/shard_map/all_to_all | solution.py:359
  150.7 1.0 couple.1
  151.7 4.8 %all-to-all-start.2 = ((bf16[128,8,256]{2,1,0:T(8,128)(2,1)}), bf16[128,8,256]{2,1,0:T(8,128)(2,1)S(1)}, u32[]{:S(2)}, u32[]{:S(2)}) async-start(bf16[128,8,256]{2,1,0:T(8,128)(2,1)} %couple.1), calls=%async_computation.2 | async-start | bytes 1048576 | tf_op jit(solution)/shard_map/all_to_all | solution.py:359
  156.4 0.0 copy-done.6
  156.5 0.1 copy.19
  156.6 0.7 copy.21.pot_ref
  157.4 12.5 %all-to-all-done.2 = bf16[128,8,256]{2,1,0:T(8,128)(2,1)S(1)} async-done(((bf16[128,8,256]{2,1,0:T(8,128)(2,1)}), bf16[128,8,256]{2,1,0:T(8,128)(2,1)S(1)}, u32[]{:S(2)}, u32[]{:S(2)}) %all-to-all-start.2) | async-done | bytes 524320 | tf_op jit(solution)/shard_map/all_to_all | solution.py:359
  169.9 0.0 copy-start.5
  169.9 0.8 copy-done.5
  170.7 12.2 %act.1 = bf16[128,240,128]{2,1,0:T(8,128)(2,1)S(1)} custom-call(s32[120]{0:T(128)} %reshape.27.groups_ref, bf16[16,64,256]{2,1,0:T(8,128)(2,1)} %bitcast.21, bf16[128,240,128]{2,1,0:T(8,128)(2,1)} %all-to-all-done.bricks_ref, bf16[30,256,512]{2,1,0:T(8,128)(2,1)} %bitcast.17, f32[30,1,512]{2,1,0:T(1,128)} %copy.21.pot_ref), custom_call_target="tpu_custom_call" | custom-call | tf_op jit(solution)/shard_map/act/pallas_call | solution.py:255
  182.9 0.0 copy-start.2
  183.0 0.0 copy-start.3
  183.0 0.0 copy-start.4
  183.0 97.4 %all_to_all.20 = bf16[128,240,128]{2,1,0:T(8,128)(2,1)} all-to-all(bf16[128,240,128]{2,1,0:T(8,128)(2,1)S(1)} %act.1), channel_id=1, replica_groups=mesh['band'=16,'slab'=8] {'slab','band'}, dimensions={0} | all-to-all | bytes 15728640 | tf_op jit(solution)/shard_map/all_to_all | solution.py:359
  280.4 0.0 copy-done.2
  280.4 0.0 copy-done.3
  280.4 0.0 copy-done.4
  280.4 0.0 copy-start.1
  280.4 14.4 %to_waves.1 = bf16[2,1,64,240,128]{4,3,2,1,0:T(8,128)(2,1)} custom-call(bf16[8,16,240,128]{3,2,1,0:T(8,128)(2,1)} %bitcast.18, bf16[2,1,64,240,128]{4,3,2,1,0:T(8,128)(2,1)} %above_ref.1, bf16[2,1,64,240,128]{4,3,2,1,0:T(8,128)(2,1)} %above_ref.1, bf16[2,1,64,240,128]{4,3,2,1,0:T(8,128)(2,1)} %above_ref.1, bf16[2,240,240]{2,1,0:T(8,128)(2,1)S(1)} %copy-done.3, ...), custom_call_target="tpu_custom_call" | custom-call | tf_op jit(solution)/shard_map/to_waves/pallas_call | solution.py:338
  294.8 0.0 copy-done.1
  (1 shorter events, 0.0 us)
Async XLA Ops:
  0.0 137.4 %copy-start = (f32[128,8,8]{0,2,1:T(8,128)S(1)}, f32[128,8,8]{0,2,1:T(8,128)}, u32[]{:S(2)}) copy-start(f32[128,8,8]{0,2,1:T(8,128)} %param.15) | copy-start | bytes 98308
  12.8 11.9 %copy-start.7 = (s32[1,30,1,4]{1,3,2,0:T(4,128)S(1)}, s32[1,30,1,4]{1,3,2,0:T(4,128)}, u32[]{:S(2)}) copy-start(s32[1,30,1,4]{1,3,2,0:T(4,128)} %param.14) | copy-start | bytes 1444
  12.8 12.7 %copy-start.8 = (bf16[512,512]{1,0:T(8,128)(2,1)S(1)}, bf16[512,512]{1,0:T(8,128)(2,1)}, u32[]{:S(2)}) copy-start(bf16[512,512]{1,0:T(8,128)(2,1)} %constant.25.clone) | copy-start | bytes 1572868
  12.8 106.5 %all-to-all-start = ((bf16[128,240,128]{2,1,0:T(8,128)(2,1)}), bf16[128,240,128]{2,1,0:T(8,128)(2,1)}, u32[]{:S(2)}, u32[]{:S(2)}) async-start(bf16[128,240,128]{2,1,0:T(8,128)(2,1)} %bitcast.19), calls=%async_computation | async-start | bytes 15728640 | tf_op jit(solution)/shard_map/all_to_all | solution.py:359
  119.3 37.2 %copy-start.6 = (f32[1,30,1,512]{3,2,1,0:T(1,128)S(1)}, f32[1,30,1,512]{3,2,1,0:T(1,128)}, u32[]{:S(2)}) copy-start(f32[1,30,1,512]{3,2,1,0:T(1,128)} %param.12) | copy-start | bytes 184324
  128.8 21.9 %all-to-all-start.1 = ((bf16[128,8,256]{2,1,0:T(8,128)(2,1)}), bf16[128,8,256]{2,1,0:T(8,128)(2,1)S(1)}, u32[]{:S(2)}, u32[]{:S(2)}) async-start(bf16[128,8,256]{2,1,0:T(8,128)(2,1)} %bitcast.20), calls=%async_computation.1 | async-start | bytes 1048576 | tf_op jit(solution)/shard_map/all_to_all | solution.py:359
  151.7 18.2 %all-to-all-start.2 = ((bf16[128,8,256]{2,1,0:T(8,128)(2,1)}), bf16[128,8,256]{2,1,0:T(8,128)(2,1)S(1)}, u32[]{:S(2)}, u32[]{:S(2)}) async-start(bf16[128,8,256]{2,1,0:T(8,128)(2,1)} %couple.1), calls=%async_computation.2 | async-start | bytes 1048576 | tf_op jit(solution)/shard_map/all_to_all | solution.py:359
  169.9 0.8 copy-start.5
  182.9 97.4 %copy-start.2 = (bf16[256,256]{1,0:T(8,128)(2,1)S(1)}, bf16[256,256]{1,0:T(8,128)(2,1)}, u32[]{:S(2)}) copy-start(bf16[256,256]{1,0:T(8,128)(2,1)} %constant.26.clone.ty_ref) | copy-start | bytes 393220
  183.0 97.4 %copy-start.3 = (bf16[2,240,240]{2,1,0:T(8,128)(2,1)S(1)}, bf16[2,240,240]{2,1,0:T(8,128)(2,1)}, u32[]{:S(2)}) copy-start(bf16[2,240,240]{2,1,0:T(8,128)(2,1)} %constant.28.clone.tx_ref) | copy-start | bytes 691204
  183.0 97.4 %copy-start.4 = (f32[240,128]{1,0:T(8,128)S(1)}, f32[240,128]{1,0:T(8,128)}, u32[]{:S(2)}) copy-start(f32[240,128]{1,0:T(8,128)} %constant.29.clone.planar_ref) | copy-start | bytes 368644
  280.4 14.5 %copy-start.1 = (f32[128,8,8]{0,2,1:T(8,128)S(1)}, f32[128,8,8]{0,2,1:T(8,128)}, u32[]{:S(2)}) copy-start(f32[128,8,8]{0,2,1:T(8,128)} %param.15) | copy-start | bytes 98308

commit v4 on v3

--- a/solution.py
+++ b/solution.py
@@ -136,9 +136,9 @@
             pl.BlockSpec((2, X, X), lambda t: (0, 0, 0)),
         ],
         out_specs=pl.BlockSpec((1, NBAND, X, 128), lambda t: (behind(t), 0, 0, 0)),
-        out_shape=jax.ShapeDtypeStruct((NSLAB, NBAND, X, 128), BF16),
+        out_shape=pltpu.VMEM((NSLAB, NBAND, X, 128), BF16),
         scratch_shapes=[pltpu.VMEM((2, NBAND, BE // 2, 2 * BE, X), BF16)] * 2,
-        compiler_params=pltpu.CompilerParams(vmem_limit_bytes=60 * MIB),
+        compiler_params=pltpu.CompilerParams(vmem_limit_bytes=52 * MIB),
         name="to_grid",
     )(orbitals, ty, tx)
 
@@ -157,7 +157,7 @@
     ]
 
 
-def project_kernel(groups_ref, bricks_ref, proj_ref, sums_ref, coef_ref):
+def project_kernel(groups_ref, bricks_ref, natural_ref, turn_ref, proj_ref, sums_ref, coef_ref):
     t = pl.program_id(0)
 
     @pl.when(t == 0)
@@ -168,6 +168,7 @@
         rows = turned_rows(bricks_ref, pair)
         for low in range(2):
             b = 2 * pair + low
+            proj_ref[b] = nn(natural_ref[b], turn_ref[...]).astype(BF16)
             partial = nt(proj_ref[b], rows[low])
             for k in range(KB):
                 g = groups_ref[(2 * PROJECT_STEP * t + b) * KB + k]
@@ -178,7 +179,9 @@
         sums_ref[...] = coef_ref[...].astype(BF16)
 
 
-def project(groups, bricks, proj):
+def project(groups, bricks, natural):
+    turn = np.zeros((P_SIZE, P_SIZE))
+    turn[point_order(), np.arange(P_SIZE)] = 1.0
     return pl.pallas_call(
         project_kernel,
         grid_spec=pltpu.PrefetchScalarGridSpec(
@@ -187,14 +190,21 @@
             in_specs=[
                 pl.BlockSpec((NDEV, 16 * PROJECT_STEP, 128), lambda t, g: (0, t, 0)),
                 pl.BlockSpec((2 * PROJECT_STEP, KB * C, P_SIZE), lambda t, g: (t, 0, 0)),
+                pl.BlockSpec((P_SIZE, P_SIZE), lambda t, g: (0, 0)),
             ],
-            out_specs=pl.BlockSpec((NGROUP, C, ROWS), lambda t, g: (0, 0, 0)),
+            out_specs=[
+                pl.BlockSpec((2 * PROJECT_STEP, KB * C, P_SIZE), lambda t, g: (t, 0, 0)),
+                pl.BlockSpec((NGROUP, C, ROWS), lambda t, g: (0, 0, 0)),
+            ],
             scratch_shapes=[pltpu.VMEM((NGROUP, C, ROWS), F32)],
         ),
-        out_shape=jax.ShapeDtypeStruct((NGROUP, C, ROWS), BF16),
-        compiler_params=pltpu.CompilerParams(vmem_limit_bytes=60 * MIB),
+        out_shape=[
+            jax.ShapeDtypeStruct((XB, KB * C, P_SIZE), BF16),
+            jax.ShapeDtypeStruct((NGROUP, C, ROWS), BF16),
+        ],
+        compiler_params=pltpu.CompilerParams(vmem_limit_bytes=50 * MIB),
         name="project",
-    )(groups, bricks, proj)
+    )(groups, bricks, natural, bf16_table(turn))
 
 
 def couple_kernel(sums_ref, strength_ref, out_ref):
@@ -361,19 +371,17 @@
 
 def on_device(orbitals, potential, projector, block_group, strengths):
     groups = block_group.reshape(-1)
-    order = point_order()
-    turn = np.zeros((P_SIZE, P_SIZE), np.float32)
-    turn[order, np.arange(P_SIZE)] = 1.0
-    proj = nn(projector.reshape(XB * KB * C, P_SIZE), jnp.asarray(turn, dtype=BF16)).astype(BF16)
-    proj = proj.reshape(XB, KB * C, P_SIZE)
+    strength = lax.dynamic_slice_in_dim(strengths, lax.axis_index(ORDER), 1, 0)
+    grid, groups, strength = lax.optimization_barrier(
+        (to_grid(orbitals).reshape(NDEV, X, 128), groups, strength)
+    )
+    bricks = exchange(grid)
+    proj, sums = project(groups, bricks, projector.reshape(XB, KB * C, P_SIZE))
+    sums, potential = lax.optimization_barrier((exchange(sums.reshape(NDEV, PROJ, ROWS)), potential))
     pot = potential.reshape(XB, BE, BE, BE).transpose(0, 2, 1, 3).reshape(XB, 1, P_SIZE)
-    own = lax.axis_index(ORDER)
-    strength = lax.dynamic_slice_in_dim(strengths, own, 1, 0)
-
-    bricks = exchange(to_grid(orbitals).reshape(NDEV, X, 128))
-    sums = project(groups, bricks, proj)
-    coupled = exchange(couple(exchange(sums.reshape(NDEV, PROJ, ROWS)), strength))
-    acted = act(groups, coupled.reshape(NGROUP, C, ROWS), bricks, proj, pot)
+    coupled = exchange(couple(sums, strength)).reshape(NGROUP, C, ROWS)
+    coupled = pltpu.with_memory_space_constraint(coupled, pltpu.VMEM)
+    acted = act(groups, coupled, bricks, proj, pot)
     returned = exchange(acted).reshape(NSLAB, NBAND, X, 128)
     return to_waves(returned, orbitals)
 

time: 296 us -> 290 us (0.980)
  blocking collectives: 97.4 us -> 218 us
  waiting for transfers between devices: 99.2 us -> 12.6 us
  starting transfers between devices: 25.2 us -> 4.75 us
  local copies, waits for them, and re-layouts: 13.2 us -> 2.01 us
  matrix products: 9.77 us -> 0 us
    all_to_all x1 -> x3, blocking collectives: 97.4 us -> 218 us  [exchange(): return lax.all_to_all(array, ORDER, split_axis=0, concat_axis=0, tiled=True)]
    all_to_all x3 -> x1, waiting for transfers between devices: 99.2 us -> 12.6 us  [exchange(): return lax.all_to_all(array, ORDER, split_axis=0, concat_axis=0, tiled=True)]
    all_to_all x3 -> x1, starting transfers between devices: 25.2 us -> 4.75 us  [exchange(): return lax.all_to_all(array, ORDER, split_axis=0, concat_axis=0, tiled=True)]
    convert_element_type x1 -> x0, local copies, waits for them, and re-layouts: 10.5 us -> none  [on_device(): nn(projector.reshape(XB * KB * C, P_SIZE), jnp.asarray(turn, dtype=BF16))]
    dot_general x1 -> x0, matrix products: 9.77 us -> none  [nn(): lax.dot_general(a, b, (((1,), (0,)), ((), ())), preferred_element_type=F32)]
    pallas_call x1, Pallas kernels: 9.53 us -> 14.1 us  [project(): pl.pallas_call(project_kernel, grid_spec=pltpu.PrefetchScalarGridSpec(num...]
  transfers between devices with their start and end apart: 3 -> 1, of which waited for: 3 -> 1; matrix products, arithmetic and copies ran while one was open for 8% -> 0% of each run, Pallas kernels for 0% -> 0%
where the time goes in v4:
time: 290 us
  blocking collectives  218 us (75%)
  Pallas kernels  52.4 us (18%)
  waiting for transfers between devices  12.6 us (4%)
  starting transfers between devices  4.75 us (2%)
    all_to_all x3, blocking collectives, exchange(): return lax.all_to_all(array, ORDER, split_axis=0, concat_axis=0, tiled=True)  218 us
    pallas_call x1, Pallas kernels, to_waves(): pl.pallas_call(to_waves_kernel, grid=(NSLAB + 1,), in_specs=[pl.BlockSpec...  14.4 us
    pallas_call x1, Pallas kernels, project(): pl.pallas_call(project_kernel, grid_spec=pltpu.PrefetchScalarGridSpec(num...  14.1 us
    all_to_all x1, waiting for transfers between devices, exchange(): return lax.all_to_all(array, ORDER, split_axis=0, concat_axis=0, tiled=True)  12.6 us
    pallas_call x1, Pallas kernels, act(): pl.pallas_call(act_kernel, grid_spec=pltpu.PrefetchScalarGridSpec(num_sca...  12.1 us
    pallas_call x1, Pallas kernels, to_grid(): pl.pallas_call(to_grid_kernel, grid=(NSLAB + 1,), in_specs=[pl.BlockSpec(...  10.7 us
  transfers between devices with their start and end apart: 1, of which 1 were waited for; matrix products, arithmetic and copies ran while one was open for 0% of the time, Pallas kernels for 0%

profile of v4, /device:TPU:1, one launch (start us, length us, event | category | flops | bytes accessed | tf_op | source)
XLA Modules:
  0.0 289.8 jit_solution(3921435822259329344)
XLA Ops:
  0.0 0.0 copy-start
  0.0 0.8 copy.15
  0.8 0.1 reshape.25.groups_ref
  0.9 0.0 copy-start.5
  0.9 0.0 copy-done
  0.9 0.1 constant_dynamic-slice_fusion
  1.0 0.1 copy.20.strength_ref
  1.1 10.7 %to_grid.1 = bf16[8,16,240,128]{3,2,1,0:T(8,128)(2,1)S(1)} custom-call(bf16[2,1,64,240,128]{4,3,2,1,0:T(8,128)(2,1)} %above_ref.1, bf16[256,256]{1,0:T(8,128)(2,1)} %constant.25.clone.ty_ref, bf16[2,240,240]{2,1,0:T(8,128)(2,1)} %constant.26.clone.tx_ref), custom_call_target="tpu_custom_call" | custom-call | tf_op jit(solution)/shard_map/to_grid/pallas_call | solution.py:130
  11.8 0.0 copy-start.2
  11.8 103.5 %all_to_all.20.bricks_ref = bf16[128,240,128]{2,1,0:T(8,128)(2,1)} all-to-all(bf16[128,240,128]{2,1,0:T(8,128)(2,1)S(1)} %bitcast.11), channel_id=1, replica_groups=mesh['band'=16,'slab'=8] {'slab','band'}, dimensions={0} | all-to-all | bytes 15728640 | tf_op jit(solution)/shard_map/all_to_all | solution.py:369
  115.4 0.0 copy-done.5
  115.4 0.0 copy-done.2
  115.4 0.0 copy-start.6
  115.4 14.1 %project.1 = (bf16[30,256,512]{2,1,0:T(8,128)(2,1)}, bf16[16,64,256]{2,1,0:T(8,128)(2,1)S(1)}) custom-call(s32[120]{0:T(128)S(1)} %reshape.25.groups_ref, bf16[128,240,128]{2,1,0:T(8,128)(2,1)} %all_to_all.20.bricks_ref, bf16[30,256,512]{2,1,0:T(8,128)(2,1)} %bitcast.15, bf16[512,512]{1,0:T(8,128)(2,1)S(1)} %copy-done.2), custom_call_target="tpu_custom_call" | custom-call | tf_op jit(solution)/shard_map/project/pallas_call | solution.py:185
  129.5 17.3 %all_to_all.21.sums_ref = bf16[128,8,256]{2,1,0:T(8,128)(2,1)S(1)} all-to-all(bf16[128,8,256]{2,1,0:T(8,128)(2,1)S(1)} %bitcast.13), channel_id=1, replica_groups=mesh['band'=16,'slab'=8] {'slab','band'}, dimensions={0} | all-to-all | bytes 1048576 | tf_op jit(solution)/shard_map/all_to_all | solution.py:369
  146.7 1.0 couple.1
  147.8 4.7 %all-to-all-start.2 = ((bf16[128,8,256]{2,1,0:T(8,128)(2,1)}), bf16[128,8,256]{2,1,0:T(8,128)(2,1)S(1)}, u32[]{:S(2)}, u32[]{:S(2)}) async-start(bf16[128,8,256]{2,1,0:T(8,128)(2,1)} %couple.1), calls=%async_computation.2 | async-start | bytes 1048576 | tf_op jit(solution)/shard_map/all_to_all | solution.py:369
  152.5 0.0 copy-done.6
  152.5 0.1 copy.17
  152.7 0.7 copy.19.pot_ref
  153.4 12.6 %all-to-all-done.2 = bf16[128,8,256]{2,1,0:T(8,128)(2,1)S(1)} async-done(((bf16[128,8,256]{2,1,0:T(8,128)(2,1)}), bf16[128,8,256]{2,1,0:T(8,128)(2,1)S(1)}, u32[]{:S(2)}, u32[]{:S(2)}) %all-to-all-start.2) | async-done | bytes 524320 | tf_op jit(solution)/shard_map/all_to_all | solution.py:369
  166.0 12.1 %act.1 = bf16[128,240,128]{2,1,0:T(8,128)(2,1)S(1)} custom-call(s32[120]{0:T(128)} %copy-done.5, bf16[16,64,256]{2,1,0:T(8,128)(2,1)S(1)} %bitcast.12, bf16[128,240,128]{2,1,0:T(8,128)(2,1)} %all_to_all.20.bricks_ref, bf16[30,256,512]{2,1,0:T(8,128)(2,1)} %get-tuple-element.17.proj_ref, f32[30,1,512]{2,1,0:T(1,128)} %copy.19.pot_ref), custom_call_target="tpu_custom_call" | custom-call | tf_op jit(solution)/shard_map/act/pallas_call | solution.py:265
  178.1 0.0 copy-start.1
  178.1 0.0 copy-start.3
  178.1 0.0 copy-start.4
  178.1 97.2 %all_to_all.22 = bf16[128,240,128]{2,1,0:T(8,128)(2,1)} all-to-all(bf16[128,240,128]{2,1,0:T(8,128)(2,1)S(1)} %act.1), channel_id=1, replica_groups=mesh['band'=16,'slab'=8] {'slab','band'}, dimensions={0} | all-to-all | bytes 15728640 | tf_op jit(solution)/shard_map/all_to_all | solution.py:369
  275.3 0.0 copy-done.1
  275.3 0.0 copy-done.3
  275.3 0.0 copy-done.4
  275.3 14.4 %to_waves.1 = bf16[2,1,64,240,128]{4,3,2,1,0:T(8,128)(2,1)} custom-call(bf16[8,16,240,128]{3,2,1,0:T(8,128)(2,1)} %bitcast.14, bf16[2,1,64,240,128]{4,3,2,1,0:T(8,128)(2,1)} %above_ref.1, bf16[2,1,64,240,128]{4,3,2,1,0:T(8,128)(2,1)} %above_ref.1, bf16[2,1,64,240,128]{4,3,2,1,0:T(8,128)(2,1)} %above_ref.1, bf16[2,240,240]{2,1,0:T(8,128)(2,1)S(1)} %copy-done.3, ...), custom_call_target="tpu_custom_call" | custom-call | tf_op jit(solution)/shard_map/to_waves/pallas_call | solution.py:348
  (1 shorter events, 0.0 us)
Async XLA Ops:
  0.0 0.9 copy-start
  0.9 114.5 %copy-start.5 = (s32[120]{0:T(128)}, s32[120]{0:T(128)S(1)}, u32[]{:S(2)}) copy-start(s32[120]{0:T(128)S(1)} %reshape.25.groups_ref) | copy-start | bytes 1444
  11.8 103.5 %copy-start.2 = (bf16[512,512]{1,0:T(8,128)(2,1)S(1)}, bf16[512,512]{1,0:T(8,128)(2,1)}, u32[]{:S(2)}) copy-start(bf16[512,512]{1,0:T(8,128)(2,1)} %constant.27.clone.turn_ref) | copy-start | bytes 1572868
  115.4 37.2 %copy-start.6 = (f32[1,30,1,512]{3,2,1,0:T(1,128)S(1)}, f32[1,30,1,512]{3,2,1,0:T(1,128)}, u32[]{:S(2)}) copy-start(f32[1,30,1,512]{3,2,1,0:T(1,128)} %param.12) | copy-start | bytes 184324
  147.8 18.2 %all-to-all-start.2 = ((bf16[128,8,256]{2,1,0:T(8,128)(2,1)}), bf16[128,8,256]{2,1,0:T(8,128)(2,1)S(1)}, u32[]{:S(2)}, u32[]{:S(2)}) async-start(bf16[128,8,256]{2,1,0:T(8,128)(2,1)} %couple.1), calls=%async_computation.2 | async-start | bytes 1048576 | tf_op jit(solution)/shard_map/all_to_all | solution.py:369
  178.1 97.2 %copy-start.1 = (bf16[256,256]{1,0:T(8,128)(2,1)S(1)}, bf16[256,256]{1,0:T(8,128)(2,1)}, u32[]{:S(2)}) copy-start(bf16[256,256]{1,0:T(8,128)(2,1)} %constant.25.clone.ty_ref) | copy-start | bytes 393220
  178.1 97.2 %copy-start.3 = (bf16[2,240,240]{2,1,0:T(8,128)(2,1)S(1)}, bf16[2,240,240]{2,1,0:T(8,128)(2,1)}, u32[]{:S(2)}) copy-start(bf16[2,240,240]{2,1,0:T(8,128)(2,1)} %constant.28.clone.tx_ref) | copy-start | bytes 691204
  178.1 97.2 %copy-start.4 = (f32[240,128]{1,0:T(8,128)S(1)}, f32[240,128]{1,0:T(8,128)}, u32[]{:S(2)}) copy-start(f32[240,128]{1,0:T(8,128)} %constant.29.clone.planar_ref) | copy-start | bytes 368644

commit v5 on v4

--- a/solution.py
+++ b/solution.py
@@ -26,7 +26,7 @@
 NGROUP = 16
 ROWS = 2 * NDEV
 HALF = 64
-STEP = 3
+STEP = 5
 PROJECT_STEP = 5
 PLANES = 4
 KINETIC_SCALE = 8.0
@@ -360,7 +360,7 @@
         out_specs=pl.BlockSpec((2, 1, BE, X, Y), lambda t: (0, 0, behind(t), 0, 0)),
         out_shape=jax.ShapeDtypeStruct((2, 1, NZ, X, Y), BF16),
         scratch_shapes=[pltpu.VMEM((2, BE, NBAND // 2, 2 * BE, X), BF16)] * 2,
-        compiler_params=pltpu.CompilerParams(vmem_limit_bytes=48 * MIB),
+        compiler_params=pltpu.CompilerParams(vmem_limit_bytes=52 * MIB),
         name="to_waves",
     )(grid, orbitals, orbitals, orbitals, tx, ty, planar)
 
@@ -383,6 +383,7 @@
     coupled = pltpu.with_memory_space_constraint(coupled, pltpu.VMEM)
     acted = act(groups, coupled, bricks, proj, pot)
     returned = exchange(acted).reshape(NSLAB, NBAND, X, 128)
+    returned = pltpu.with_memory_space_constraint(returned, pltpu.VMEM)
     return to_waves(returned, orbitals)
 
 

time: 290 us -> 293 us (1.010)
  local copies, waits for them, and re-layouts: 2.01 us -> 5.21 us
    unnamed x15 -> x11, local copies, waits for them, and re-layouts: 0.82 us -> 4.01 us
where the time goes in v5:
time: 293 us; the launch traced here: 292 us
  blocking collectives  218 us (74%)
  Pallas kernels  51.1 us (17%)
  waiting for transfers between devices  12.6 us (4%)
  local copies, waits for them, and re-layouts  5.21 us (2%)
  starting transfers between devices  4.75 us (2%)
    all_to_all x3, blocking collectives, exchange(): return lax.all_to_all(array, ORDER, split_axis=0, concat_axis=0, tiled=True)  218 us
    pallas_call x1, Pallas kernels, project(): pl.pallas_call(project_kernel, grid_spec=pltpu.PrefetchScalarGridSpec(num...  14 us
    pallas_call x1, Pallas kernels, to_waves(): pl.pallas_call(to_waves_kernel, grid=(NSLAB + 1,), in_specs=[pl.BlockSpec...  13.3 us
    all_to_all x1, waiting for transfers between devices, exchange(): return lax.all_to_all(array, ORDER, split_axis=0, concat_axis=0, tiled=True)  12.6 us
    pallas_call x1, Pallas kernels, act(): pl.pallas_call(act_kernel, grid_spec=pltpu.PrefetchScalarGridSpec(num_sca...  12.1 us
    pallas_call x1, Pallas kernels, to_grid(): pl.pallas_call(to_grid_kernel, grid=(NSLAB + 1,), in_specs=[pl.BlockSpec(...  10.7 us
  transfers between devices with their start and end apart: 1, of which 1 were waited for; matrix products, arithmetic and copies ran while one was open for 0% of the time, Pallas kernels for 0%

profile of v5, /device:TPU:1, one launch (start us, length us, event | category | flops | bytes accessed | tf_op | source)
XLA Modules:
  0.0 292.0 jit_solution(4136585646448090965)
XLA Ops:
  0.0 0.0 copy-start
  0.0 0.8 copy.15
  0.8 0.1 reshape.25.groups_ref
  0.9 0.0 copy-start.3
  0.9 0.0 copy-done
  0.9 0.1 constant_dynamic-slice_fusion
  1.0 0.1 copy.20.strength_ref
  1.1 10.7 %to_grid.1 = bf16[8,16,240,128]{3,2,1,0:T(8,128)(2,1)S(1)} custom-call(bf16[2,1,64,240,128]{4,3,2,1,0:T(8,128)(2,1)} %above_ref.1, bf16[256,256]{1,0:T(8,128)(2,1)} %constant.25.clone.ty_ref, bf16[2,240,240]{2,1,0:T(8,128)(2,1)} %constant.26.clone.tx_ref), custom_call_target="tpu_custom_call" | custom-call | tf_op jit(solution)/shard_map/to_grid/pallas_call | solution.py:130
  11.8 0.0 copy-start.2
  11.8 103.5 %all_to_all.20.bricks_ref = bf16[128,240,128]{2,1,0:T(8,128)(2,1)} all-to-all(bf16[128,240,128]{2,1,0:T(8,128)(2,1)S(1)} %bitcast.12), channel_id=1, replica_groups=mesh['band'=16,'slab'=8] {'slab','band'}, dimensions={0} | all-to-all | bytes 15728640 | tf_op jit(solution)/shard_map/all_to_all | solution.py:369
  115.4 0.0 copy-done.3
  115.4 0.0 copy-done.2
  115.4 0.0 copy-start.4
  115.4 14.0 %project.1 = (bf16[30,256,512]{2,1,0:T(8,128)(2,1)}, bf16[16,64,256]{2,1,0:T(8,128)(2,1)S(1)}) custom-call(s32[120]{0:T(128)S(1)} %reshape.25.groups_ref, bf16[128,240,128]{2,1,0:T(8,128)(2,1)} %all_to_all.20.bricks_ref, bf16[30,256,512]{2,1,0:T(8,128)(2,1)} %bitcast.15, bf16[512,512]{1,0:T(8,128)(2,1)S(1)} %copy-done.2), custom_call_target="tpu_custom_call" | custom-call | tf_op jit(solution)/shard_map/project/pallas_call | solution.py:185
  129.3 17.3 %all_to_all.21.sums_ref = bf16[128,8,256]{2,1,0:T(8,128)(2,1)S(1)} all-to-all(bf16[128,8,256]{2,1,0:T(8,128)(2,1)S(1)} %bitcast.14), channel_id=1, replica_groups=mesh['band'=16,'slab'=8] {'slab','band'}, dimensions={0} | all-to-all | bytes 1048576 | tf_op jit(solution)/shard_map/all_to_all | solution.py:369
  146.6 1.0 couple.1
  147.6 4.7 %all-to-all-start.2 = ((bf16[128,8,256]{2,1,0:T(8,128)(2,1)}), bf16[128,8,256]{2,1,0:T(8,128)(2,1)S(1)}, u32[]{:S(2)}, u32[]{:S(2)}) async-start(bf16[128,8,256]{2,1,0:T(8,128)(2,1)} %couple.1), calls=%async_computation.2 | async-start | bytes 1048576 | tf_op jit(solution)/shard_map/all_to_all | solution.py:369
  152.4 0.0 copy-done.4
  152.4 0.1 copy.17
  152.5 0.7 copy.19.pot_ref
  153.3 12.6 %all-to-all-done.2 = bf16[128,8,256]{2,1,0:T(8,128)(2,1)S(1)} async-done(((bf16[128,8,256]{2,1,0:T(8,128)(2,1)}), bf16[128,8,256]{2,1,0:T(8,128)(2,1)S(1)}, u32[]{:S(2)}, u32[]{:S(2)}) %all-to-all-start.2) | async-done | bytes 524320 | tf_op jit(solution)/shard_map/all_to_all | solution.py:369
  165.8 12.1 %act.1 = bf16[128,240,128]{2,1,0:T(8,128)(2,1)S(1)} custom-call(s32[120]{0:T(128)} %copy-done.3, bf16[16,64,256]{2,1,0:T(8,128)(2,1)S(1)} %bitcast.13, bf16[128,240,128]{2,1,0:T(8,128)(2,1)} %all_to_all.20.bricks_ref, bf16[30,256,512]{2,1,0:T(8,128)(2,1)} %get-tuple-element.17.proj_ref, f32[30,1,512]{2,1,0:T(1,128)} %copy.19.pot_ref), custom_call_target="tpu_custom_call" | custom-call | tf_op jit(solution)/shard_map/act/pallas_call | solution.py:265
  178.0 0.0 copy-start.1
  178.0 3.2 %copy-done.1 = bf16[128,240,128]{2,1,0:T(8,128)(2,1)} copy-done((bf16[128,240,128]{2,1,0:T(8,128)(2,1)}, bf16[128,240,128]{2,1,0:T(8,128)(2,1)S(1)}, u32[]{:S(2)}) %copy-start.1) | copy-done | bytes 7864344
  181.2 97.5 %all_to_all.22 = bf16[128,240,128]{2,1,0:T(8,128)(2,1)S(1)} all-to-all(bf16[128,240,128]{2,1,0:T(8,128)(2,1)} %copy-done.1), channel_id=1, replica_groups=mesh['band'=16,'slab'=8] {'slab','band'}, dimensions={0} | all-to-all | bytes 15728640 | tf_op jit(solution)/shard_map/all_to_all | solution.py:369
  278.7 13.3 %to_waves.1 = bf16[2,1,64,240,128]{4,3,2,1,0:T(8,128)(2,1)} custom-call(bf16[8,16,240,128]{3,2,1,0:T(8,128)(2,1)S(1)} %bitcast.11, bf16[2,1,64,240,128]{4,3,2,1,0:T(8,128)(2,1)} %above_ref.1, bf16[2,1,64,240,128]{4,3,2,1,0:T(8,128)(2,1)} %above_ref.1, bf16[2,1,64,240,128]{4,3,2,1,0:T(8,128)(2,1)} %above_ref.1, bf16[2,240,240]{2,1,0:T(8,128)(2,1)} %constant.28.clone.tx_ref, ...), custom_call_target="tpu_custom_call" | custom-call | tf_op jit(solution)/shard_map/to_waves/pallas_call | solution.py:348
  (1 shorter events, 0.0 us)
Async XLA Ops:
  0.0 0.9 copy-start
  0.9 114.5 %copy-start.3 = (s32[120]{0:T(128)}, s32[120]{0:T(128)S(1)}, u32[]{:S(2)}) copy-start(s32[120]{0:T(128)S(1)} %reshape.25.groups_ref) | copy-start | bytes 1444
  11.8 103.5 %copy-start.2 = (bf16[512,512]{1,0:T(8,128)(2,1)S(1)}, bf16[512,512]{1,0:T(8,128)(2,1)}, u32[]{:S(2)}) copy-start(bf16[512,512]{1,0:T(8,128)(2,1)} %constant.27.clone.turn_ref) | copy-start | bytes 1572868
  115.4 37.0 %copy-start.4 = (f32[1,30,1,512]{3,2,1,0:T(1,128)S(1)}, f32[1,30,1,512]{3,2,1,0:T(1,128)}, u32[]{:S(2)}) copy-start(f32[1,30,1,512]{3,2,1,0:T(1,128)} %param.12) | copy-start | bytes 184324
  147.6 18.2 %all-to-all-start.2 = ((bf16[128,8,256]{2,1,0:T(8,128)(2,1)}), bf16[128,8,256]{2,1,0:T(8,128)(2,1)S(1)}, u32[]{:S(2)}, u32[]{:S(2)}) async-start(bf16[128,8,256]{2,1,0:T(8,128)(2,1)} %couple.1), calls=%async_computation.2 | async-start | bytes 1048576 | tf_op jit(solution)/shard_map/all_to_all | solution.py:369
  178.0 3.2 %copy-start.1 = (bf16[128,240,128]{2,1,0:T(8,128)(2,1)}, bf16[128,240,128]{2,1,0:T(8,128)(2,1)S(1)}, u32[]{:S(2)}) copy-start(bf16[128,240,128]{2,1,0:T(8,128)(2,1)S(1)} %act.1) | copy-start | bytes 23592964

commit v6 on v4

--- a/solution.py
+++ b/solution.py
@@ -26,7 +26,7 @@
 NGROUP = 16
 ROWS = 2 * NDEV
 HALF = 64
-STEP = 3
+STEP = 5
 PROJECT_STEP = 5
 PLANES = 4
 KINETIC_SCALE = 8.0

time: 290 us -> 291 us (level)
  no operation moved by 1% of the time
where the time goes in v6:
time: 291 us; the launch traced here: 290 us
  blocking collectives  218 us (75%)
  Pallas kernels  52.4 us (18%)
  waiting for transfers between devices  12.6 us (4%)
  starting transfers between devices  4.75 us (2%)
    all_to_all x3, blocking collectives, exchange(): return lax.all_to_all(array, ORDER, split_axis=0, concat_axis=0, tiled=True)  218 us
    pallas_call x1, Pallas kernels, to_waves(): pl.pallas_call(to_waves_kernel, grid=(NSLAB + 1,), in_specs=[pl.BlockSpec...  14.4 us
    pallas_call x1, Pallas kernels, project(): pl.pallas_call(project_kernel, grid_spec=pltpu.PrefetchScalarGridSpec(num...  14.1 us
    all_to_all x1, waiting for transfers between devices, exchange(): return lax.all_to_all(array, ORDER, split_axis=0, concat_axis=0, tiled=True)  12.6 us
    pallas_call x1, Pallas kernels, act(): pl.pallas_call(act_kernel, grid_spec=pltpu.PrefetchScalarGridSpec(num_sca...  12.1 us
    pallas_call x1, Pallas kernels, to_grid(): pl.pallas_call(to_grid_kernel, grid=(NSLAB + 1,), in_specs=[pl.BlockSpec(...  10.7 us
  transfers between devices with their start and end apart: 1, of which 1 were waited for; matrix products, arithmetic and copies ran while one was open for 0% of the time, Pallas kernels for 0%

profile of v6, /device:TPU:1, one launch (start us, length us, event | category | flops | bytes accessed | tf_op | source)
XLA Modules:
  0.0 290.0 jit_solution(6770621291506826849)
XLA Ops:
  0.0 0.0 copy-start
  0.0 0.8 copy.15
  0.8 0.1 reshape.25.groups_ref
  0.9 0.0 copy-start.5
  0.9 0.0 copy-done
  0.9 0.1 constant_dynamic-slice_fusion
  1.0 0.1 copy.20.strength_ref
  1.1 10.7 %to_grid.1 = bf16[8,16,240,128]{3,2,1,0:T(8,128)(2,1)S(1)} custom-call(bf16[2,1,64,240,128]{4,3,2,1,0:T(8,128)(2,1)} %above_ref.1, bf16[256,256]{1,0:T(8,128)(2,1)} %constant.25.clone.ty_ref, bf16[2,240,240]{2,1,0:T(8,128)(2,1)} %constant.26.clone.tx_ref), custom_call_target="tpu_custom_call" | custom-call | tf_op jit(solution)/shard_map/to_grid/pallas_call | solution.py:130
  11.8 0.0 copy-start.2
  11.8 103.5 %all_to_all.20.bricks_ref = bf16[128,240,128]{2,1,0:T(8,128)(2,1)} all-to-all(bf16[128,240,128]{2,1,0:T(8,128)(2,1)S(1)} %bitcast.11), channel_id=1, replica_groups=mesh['band'=16,'slab'=8] {'slab','band'}, dimensions={0} | all-to-all | bytes 15728640 | tf_op jit(solution)/shard_map/all_to_all | solution.py:369
  115.4 0.0 copy-done.5
  115.4 0.0 copy-done.2
  115.4 0.0 copy-start.6
  115.4 14.1 %project.1 = (bf16[30,256,512]{2,1,0:T(8,128)(2,1)}, bf16[16,64,256]{2,1,0:T(8,128)(2,1)S(1)}) custom-call(s32[120]{0:T(128)S(1)} %reshape.25.groups_ref, bf16[128,240,128]{2,1,0:T(8,128)(2,1)} %all_to_all.20.bricks_ref, bf16[30,256,512]{2,1,0:T(8,128)(2,1)} %bitcast.15, bf16[512,512]{1,0:T(8,128)(2,1)S(1)} %copy-done.2), custom_call_target="tpu_custom_call" | custom-call | tf_op jit(solution)/shard_map/project/pallas_call | solution.py:185
  129.5 17.3 %all_to_all.21.sums_ref = bf16[128,8,256]{2,1,0:T(8,128)(2,1)S(1)} all-to-all(bf16[128,8,256]{2,1,0:T(8,128)(2,1)S(1)} %bitcast.13), channel_id=1, replica_groups=mesh['band'=16,'slab'=8] {'slab','band'}, dimensions={0} | all-to-all | bytes 1048576 | tf_op jit(solution)/shard_map/all_to_all | solution.py:369
  146.7 1.0 couple.1
  147.8 4.7 %all-to-all-start.2 = ((bf16[128,8,256]{2,1,0:T(8,128)(2,1)}), bf16[128,8,256]{2,1,0:T(8,128)(2,1)S(1)}, u32[]{:S(2)}, u32[]{:S(2)}) async-start(bf16[128,8,256]{2,1,0:T(8,128)(2,1)} %couple.1), calls=%async_computation.2 | async-start | bytes 1048576 | tf_op jit(solution)/shard_map/all_to_all | solution.py:369
  152.5 0.0 copy-done.6
  152.5 0.1 copy.17
  152.7 0.7 copy.19.pot_ref
  153.4 12.6 %all-to-all-done.2 = bf16[128,8,256]{2,1,0:T(8,128)(2,1)S(1)} async-done(((bf16[128,8,256]{2,1,0:T(8,128)(2,1)}), bf16[128,8,256]{2,1,0:T(8,128)(2,1)S(1)}, u32[]{:S(2)}, u32[]{:S(2)}) %all-to-all-start.2) | async-done | bytes 524320 | tf_op jit(solution)/shard_map/all_to_all | solution.py:369
  166.0 12.1 %act.1 = bf16[128,240,128]{2,1,0:T(8,128)(2,1)S(1)} custom-call(s32[120]{0:T(128)} %copy-done.5, bf16[16,64,256]{2,1,0:T(8,128)(2,1)S(1)} %bitcast.12, bf16[128,240,128]{2,1,0:T(8,128)(2,1)} %all_to_all.20.bricks_ref, bf16[30,256,512]{2,1,0:T(8,128)(2,1)} %get-tuple-element.17.proj_ref, f32[30,1,512]{2,1,0:T(1,128)} %copy.19.pot_ref), custom_call_target="tpu_custom_call" | custom-call | tf_op jit(solution)/shard_map/act/pallas_call | solution.py:265
  178.1 0.0 copy-start.1
  178.1 0.0 copy-start.3
  178.1 0.0 copy-start.4
  178.2 97.4 %all_to_all.22 = bf16[128,240,128]{2,1,0:T(8,128)(2,1)} all-to-all(bf16[128,240,128]{2,1,0:T(8,128)(2,1)S(1)} %act.1), channel_id=1, replica_groups=mesh['band'=16,'slab'=8] {'slab','band'}, dimensions={0} | all-to-all | bytes 15728640 | tf_op jit(solution)/shard_map/all_to_all | solution.py:369
  275.5 0.0 copy-done.1
  275.5 0.0 copy-done.3
  275.5 0.0 copy-done.4
  275.5 14.4 %to_waves.1 = bf16[2,1,64,240,128]{4,3,2,1,0:T(8,128)(2,1)} custom-call(bf16[8,16,240,128]{3,2,1,0:T(8,128)(2,1)} %bitcast.14, bf16[2,1,64,240,128]{4,3,2,1,0:T(8,128)(2,1)} %above_ref.1, bf16[2,1,64,240,128]{4,3,2,1,0:T(8,128)(2,1)} %above_ref.1, bf16[2,1,64,240,128]{4,3,2,1,0:T(8,128)(2,1)} %above_ref.1, bf16[2,240,240]{2,1,0:T(8,128)(2,1)S(1)} %copy-done.3, ...), custom_call_target="tpu_custom_call" | custom-call | tf_op jit(solution)/shard_map/to_waves/pallas_call | solution.py:348
  (1 shorter events, 0.0 us)
Async XLA Ops:
  0.0 0.9 copy-start
  0.9 114.5 %copy-start.5 = (s32[120]{0:T(128)}, s32[120]{0:T(128)S(1)}, u32[]{:S(2)}) copy-start(s32[120]{0:T(128)S(1)} %reshape.25.groups_ref) | copy-start | bytes 1444
  11.8 103.5 %copy-start.2 = (bf16[512,512]{1,0:T(8,128)(2,1)S(1)}, bf16[512,512]{1,0:T(8,128)(2,1)}, u32[]{:S(2)}) copy-start(bf16[512,512]{1,0:T(8,128)(2,1)} %constant.27.clone.turn_ref) | copy-start | bytes 1572868
  115.4 37.2 %copy-start.6 = (f32[1,30,1,512]{3,2,1,0:T(1,128)S(1)}, f32[1,30,1,512]{3,2,1,0:T(1,128)}, u32[]{:S(2)}) copy-start(f32[1,30,1,512]{3,2,1,0:T(1,128)} %param.12) | copy-start | bytes 184324
  147.8 18.2 %all-to-all-start.2 = ((bf16[128,8,256]{2,1,0:T(8,128)(2,1)}), bf16[128,8,256]{2,1,0:T(8,128)(2,1)S(1)}, u32[]{:S(2)}, u32[]{:S(2)}) async-start(bf16[128,8,256]{2,1,0:T(8,128)(2,1)} %couple.1), calls=%async_computation.2 | async-start | bytes 1048576 | tf_op jit(solution)/shard_map/all_to_all | solution.py:369
  178.1 97.4 %copy-start.1 = (bf16[256,256]{1,0:T(8,128)(2,1)S(1)}, bf16[256,256]{1,0:T(8,128)(2,1)}, u32[]{:S(2)}) copy-start(bf16[256,256]{1,0:T(8,128)(2,1)} %constant.25.clone.ty_ref) | copy-start | bytes 393220
  178.1 97.4 %copy-start.3 = (bf16[2,240,240]{2,1,0:T(8,128)(2,1)S(1)}, bf16[2,240,240]{2,1,0:T(8,128)(2,1)}, u32[]{:S(2)}) copy-start(bf16[2,240,240]{2,1,0:T(8,128)(2,1)} %constant.28.clone.tx_ref) | copy-start | bytes 691204
  178.1 97.4 %copy-start.4 = (f32[240,128]{1,0:T(8,128)S(1)}, f32[240,128]{1,0:T(8,128)}, u32[]{:S(2)}) copy-start(f32[240,128]{1,0:T(8,128)} %constant.29.clone.planar_ref) | copy-start | bytes 368644
